TPU v7x, 32 devices: a whole 2x2x4 slice. The times are simulated.
32 devices in a mesh: skyx: 4 (over y, core), skyy: 8 (over z, x).
Axes of the slice: x: 2, y: 2, z: 4, core: 2. Of those that a mesh axis runs over, the one named last changes fastest.
Arguments:
- image: bfloat16 [512, 16, 512], P(('skyx', 'skyy')), may hold values from -6 to 6
- inverse_var: bfloat16 [512, 16, 512], P(('skyx', 'skyy')), may hold values from 0.099609375 to 1
- patch_of: int32 [512, 1], replicated, may hold values from 0 to 31; in each aligned block of 16 rows (0 to 15, 16 to 31, ...) no two rows name the same one
- row_of: int32 [512], replicated, may hold values from 0 to 3
- valid: int32 [512], replicated, may hold values 0 or 1
- coef_index: int32 [32], replicated, may hold values from 0 to 63
- coef_table: float32 [64, 20], replicated, may hold values from -1.25 to 1.25
- basis_across: float32 [20, 41], replicated, may hold values from -1 to 1
- basis_down: float32 [20, 41], replicated, may hold values from -1 to 1
Outputs:
- coadd: float32 [512, 2048], P('skyy', 'skyx')
- weight_sum: float32 [512, 2048], P('skyy', 'skyx')
Inputs may be any that keep to these rules, and one draw needn't show every extreme that they name: `patch_of`: within the 16 blocks of one exposure (the rows of one device) no patch appears twice.
All inputs are finite; a program needn't handle non-finite values.
Results may differ from a plain program's by a relative error of at most 0.0065.
Values may be sent and summed in bfloat16 or wider, within the bound.
A program may use at most 192 MiB of HBM per device.

v0:
```python
import jax
import jax.numpy as jnp
from jax import lax
from jax.sharding import PartitionSpec as P

RS = 4


group_blocks = 8


def from_behind(value, axis, steps):
    count = lax.axis_size(axis)
    initial, last = (max(0, -steps), min(count, count - steps))
    return lax.ppermute(value, axis, [(source, source + steps) for source in range(initial, last)])


def band_pair(basis_across):
    margin = (basis_across.shape[1] - 1) // 2
    rows_in = jnp.arange(128, dtype=jnp.int32)[:, None]
    cols_out = jnp.arange(128, dtype=jnp.int32)[None, :]
    offset_now = cols_out - rows_in
    offset_prev = cols_out + 128 - rows_in
    inside_now = (offset_now >= 0) & (offset_now <= 2 * margin)
    inside_prev = (offset_prev >= 0) & (offset_prev <= 2 * margin)
    band_now = jnp.where(
        inside_now[None], jnp.take(basis_across, jnp.clip(offset_now, 0, 2 * margin), axis=1), 0.0
    )
    band_prev = jnp.where(
        inside_prev[None], jnp.take(basis_across, jnp.clip(offset_prev, 0, 2 * margin), axis=1), 0.0
    )
    return (band_now.astype(jnp.bfloat16), band_prev.astype(jnp.bfloat16))


def vertical_mix(basis_down, coeffs, row_count):
    margin = (basis_down.shape[1] - 1) // 2
    rows_out = jnp.arange(row_count + 2 * margin, dtype=jnp.int32)[:, None]
    rows_in = jnp.arange(row_count, dtype=jnp.int32)[None, :]
    offset = rows_out - rows_in
    inside = (offset >= 0) & (offset <= 2 * margin)
    picked = jnp.where(
        inside[None], jnp.take(basis_down, jnp.clip(offset, 0, 2 * margin), axis=1), 0.0
    )
    mixed_taps = coeffs[:, :, None, None] * picked[None]
    mixed_taps = jnp.transpose(mixed_taps, (0, 2, 1, 3))
    return mixed_taps.reshape(mixed_taps.shape[0], row_count + 2 * margin, -1).astype(jnp.bfloat16)


def convolve(planes, coeffs, bands, basis_down, out_width):
    block_count, row_count, block_width = planes.shape
    band_now, band_prev = bands
    tile_count = out_width // 128
    padded = jnp.pad(planes, ((0, 0), (0, 0), (128, out_width - block_width)))
    tiles = padded.reshape(block_count, row_count, tile_count + 1, 128)
    swept_rows = jnp.einsum(
        "krti,cio->kcrto", tiles[:, :, 1:], band_now, preferred_element_type=jnp.float32
    )
    swept_rows = swept_rows + jnp.einsum(
        "krti,cio->kcrto", tiles[:, :, :tile_count], band_prev, preferred_element_type=jnp.float32
    )
    swept_rows = swept_rows.astype(jnp.bfloat16).reshape(block_count, -1, out_width)
    mixer_taps = vertical_mix(basis_down, coeffs, row_count)
    return jnp.einsum(
        "kyj,kjx->kyx", mixer_taps, swept_rows, preferred_element_type=jnp.float32
    ).astype(jnp.bfloat16)


def deliver(first_plane, second_plane):
    return (
        lax.all_to_all(first_plane, ("skyx", "skyy"), split_axis=0, concat_axis=0, tiled=True),
        lax.all_to_all(second_plane, ("skyx", "skyy"), split_axis=0, concat_axis=0, tiled=True),
    )


def route_planes(route_onehot, planes):
    return jnp.einsum(
        "kd,krx->drx", route_onehot, planes, preferred_element_type=jnp.float32
    ).astype(jnp.bfloat16)


def body(
    image, inverse_var, patch_of, row_of, valid, coef_index, coef_table, basis_across, basis_down
):
    devices = lax.axis_size("skyx") * lax.axis_size("skyy")
    block_count, row_count, block_width = image.shape
    margin = (basis_across.shape[1] - 1) // 2
    out_width = (block_width + 2 * margin + 127) // 128 * 128
    patch_rows = RS * row_count
    my_patch = lax.axis_index("skyx") * lax.axis_size("skyy") + lax.axis_index("skyy")
    first_row = my_patch * block_count
    my_valid = lax.dynamic_slice_in_dim(valid, first_row, block_count)
    my_targets = lax.dynamic_slice_in_dim(patch_of[:, 0], first_row, block_count)
    valid_flags = my_valid.astype(jnp.float32)[:, None, None]
    kept_planes = (valid_flags * inverse_var.astype(jnp.float32)).astype(jnp.bfloat16)
    weighted = (valid_flags * inverse_var.astype(jnp.float32) * image.astype(jnp.float32)).astype(
        jnp.bfloat16
    )
    choose = (
        coef_index[:, None] == jnp.arange(coef_table.shape[0], dtype=jnp.int32)[None, :]
    ).astype(jnp.float32)
    coeffs = jnp.dot(choose, coef_table, precision=lax.Precision.HIGHEST)
    bands = band_pair(basis_across)
    target_grid = patch_of[:, 0].reshape(devices, block_count)
    slot_grid = row_of.reshape(devices, block_count)
    hits = target_grid == my_patch
    has_block = jnp.any(hits, axis=1)
    slot_source = jnp.sum(jnp.where(hits, slot_grid, 0), axis=1)
    slot_onehot = (
        (slot_source[:, None] == jnp.arange(RS, dtype=jnp.int32)[None, :]) & has_block[:, None]
    ).astype(jnp.bfloat16)
    route_onehot = (my_targets[:, None] == jnp.arange(devices, dtype=jnp.int32)[None, :]).astype(
        jnp.bfloat16
    )
    kept_send = route_planes(route_onehot, kept_planes)
    weighted_send = route_planes(route_onehot, weighted)
    weighted_in, kept_in = deliver(weighted_send, kept_send)
    ranks = jnp.cumsum(has_block.astype(jnp.int32)) - 1
    live_count = jnp.sum(has_block.astype(jnp.int32))
    ranks = jnp.where(has_block, ranks, -1)
    turns = (live_count + group_blocks - 1) // group_blocks
    flat_in = weighted_in.reshape(devices, row_count * block_width)

    def add_group(turn, slot_state):
        wanted = turn * group_blocks + jnp.arange(group_blocks, dtype=jnp.int32)
        pick_table = wanted[:, None] == ranks[None, :]
        pick_bf = pick_table.astype(jnp.bfloat16)
        planes = jnp.dot(pick_bf, flat_in, preferred_element_type=jnp.float32).astype(jnp.bfloat16)
        planes = planes.reshape(group_blocks, row_count, block_width)
        group_coeffs = jnp.dot(
            pick_table.astype(jnp.float32), coeffs, precision=lax.Precision.HIGHEST
        )
        contrib = convolve(planes, group_coeffs, bands, basis_down, out_width)
        choose_slot = jnp.dot(pick_bf, slot_onehot, preferred_element_type=jnp.float32).astype(
            jnp.bfloat16
        )
        return slot_state + jnp.einsum(
            "gs,gyx->syx", choose_slot, contrib, preferred_element_type=jnp.float32
        )

    slot_sums = lax.fori_loop(
        0, turns, add_group, jnp.zeros((RS, row_count + 2 * margin, out_width), jnp.float32)
    )
    weight_sum = jnp.einsum(
        "ks,kyx->syx", slot_onehot, kept_in, preferred_element_type=jnp.float32
    ).reshape(patch_rows, block_width)
    extended = jnp.zeros((patch_rows + 2 * margin, out_width), jnp.float32)
    for slot_index in range(RS):
        extended = extended.at[
            slot_index * row_count : slot_index * row_count + row_count + 2 * margin
        ].add(slot_sums[slot_index])
    from_below = from_behind(extended[:margin], "skyy", -1)
    from_above = from_behind(extended[patch_rows + margin :], "skyy", 1)
    middle = extended[margin : margin + patch_rows]
    middle = middle.at[patch_rows - margin :].add(from_below)
    middle = middle.at[:margin].add(from_above)
    right_start = min(block_width + margin, out_width - 128)
    right_offset = block_width + margin - right_start
    from_right = from_behind(middle[:, :128], "skyx", -1)
    from_left = from_behind(middle[:, right_start : right_start + 128], "skyx", 1)
    coadd = middle[:, margin : margin + block_width]
    coadd = coadd.at[:, block_width - margin :].add(from_right[:, :margin])
    coadd = coadd.at[:, :margin].add(from_left[:, right_offset : right_offset + margin])
    return (coadd, weight_sum)


def solution(mesh):
    placed = (
        P(("skyx", "skyy"), None, None),
        P(("skyx", "skyy"), None, None),
        P(),
        P(),
        P(),
        P(),
        P(),
        P(),
        P(),
    )
    return jax.shard_map(
        body,
        mesh=mesh,
        in_specs=placed,
        out_specs=(P("skyy", "skyx"), P("skyy", "skyx")),
        check_vma=False,
    )
```

profile of v0, /device:TPU:20, one launch (start us, length us, event | category | flops | bytes accessed | tf_op | source)
XLA Modules:
  0.0 279.3 jit_solution(7165453357666435508)
XLA Ops:
  0.7 0.7 fusion.73
  1.4 0.8 dynamic-slice_convert_fusion
  2.2 1.2 fusion.41
  3.4 0.4 convolution_convert_fusion.4
  3.8 1.1 copy.50
  4.9 5.9 %all-to-all-start = ((bf16[32,16,512]{2,1,0:T(8,128)(2,1)}), bf16[32,16,512]{2,1,0:T(8,128)(2,1)S(1)}, u32[]{:S(2)}, u32[]{:S(2)}) async-start(bf16[32,16,512]{2,1,0:T(8,128)(2,1)} %copy.50), calls=%async_computation | async-start | bytes 1048576 | tf_op jit(solution)/shard_map/all_to_all | solution.py:70
  10.8 0.7 compare_reduce_fusion
  11.6 0.1 reduce_or.9
  11.9 0.1 add_reduce_fusion
  12.0 0.6 broadcast_select_fusion
  12.6 0.8 reshape.386
  13.4 0.1 select_reduce_fusion
  13.6 0.4 convolution_convert_fusion.3
  14.9 1.1 copy.61
  16.0 57.5 %gather_fusion.1 = bf16[16384,20]{1,0:T(8,128)(2,1)} fusion(bf16[20,41]{0,1:T(8,128)(2,1)S(1)} %copy.51, s32[16384]{0:T(1024)S(1)} %bitcast_clamp_fusion.1), kind=kCustom, calls=%fused_computation.clone | custom fusion | bytes 1376256 | tf_op jit(solution)/shard_map/jit(_take)/gather | solution.py:27
  73.5 3.9 %copy.52 = bf16[128,128,20]{1,0,2:T(8,128)(2,1)S(1)} copy(bf16[128,128,20]{2,1,0:T(8,128)(2,1)} %bitcast.111) | data formatting | bytes 1310720 | tf_op jit(solution)/shard_map/jit(_take)/gather | solution.py:27
  77.4 57.5 %gather_fusion.2 = bf16[16384,20]{1,0:T(8,128)(2,1)} fusion(bf16[20,41]{0,1:T(8,128)(2,1)S(1)} %copy.51, s32[16384]{0:T(1024)S(1)} %bitcast_clamp_fusion), kind=kCustom, calls=%fused_computation.2.clone | custom fusion | bytes 1376256 | tf_op jit(solution)/shard_map/jit(_take)/gather | solution.py:30
  134.9 3.9 %copy.54 = bf16[128,128,20]{1,0,2:T(8,128)(2,1)S(1)} copy(bf16[128,128,20]{2,1,0:T(8,128)(2,1)} %bitcast.110) | data formatting | bytes 1310720 | tf_op jit(solution)/shard_map/jit(_take)/gather | solution.py:30
  138.8 0.2 fusion.61
  139.1 1.1 fusion.38
  140.1 1.0 fusion.37
  141.2 5.9 %all-to-all-start.1 = ((bf16[32,16,512]{2,1,0:T(8,128)(2,1)}), bf16[32,16,512]{2,1,0:T(8,128)(2,1)}, u32[]{:S(2)}, u32[]{:S(2)}) async-start(bf16[32,16,512]{2,1,0:T(8,128)(2,1)} %copy.61), calls=%async_computation.1 | async-start | bytes 1048576 | tf_op jit(solution)/shard_map/all_to_all | solution.py:71
  147.1 1.1 copy.70
  148.2 0.9 broadcast_in_dim.79
  149.1 52.5 %while.21 = (s32[]{:T(128)}, f32[4,56,640]{2,0,1:T(4,128)}, s32[]{:T(128)}, s32[32]{0:T(128)S(1)}, f32[32,20]{0,1:T(8,128)S(1)}, /*index=5*/f32[20,41]{0,1:T(8,1...) while((s32[]{:T(128)}, f32[4,56,640]{2,0,1:T(4,128)}, ...), condition=%wide.region_5.7_spmd.clone, body=%wide.region_4.6_spmd.clone.sunk | while | flops 1033024640 | bytes 39710264 | solution.py:140
  149.1 0.2 fusion.110
  149.6 1.3 convolution_convert_fusion.7
  150.9 0.2 reshape.453
  151.3 1.9 gather_fusion
  153.2 0.3 copy.95
  153.6 2.1 fusion.107
  155.7 2.1 fusion.108
  157.8 6.4 %copy.94 = bf16[8,20,16,5,128]{4,3,2,1,0:T(8,128)(2,1)} copy(bf16[8,20,16,5,128]{4,2,1,3,0:T(8,128)(2,1)S(1)} %fusion.108) | data formatting | bytes 6553600 | tf_op jit(solution)/shard_map/while/body/convert_element_type | solution.py:61
  164.2 7.0 %reshape.454 = bf16[8,320,640]{2,1,0:T(8,128)(2,1)S(1)} reshape(bf16[8,20,16,5,128]{4,3,2,1,0:T(8,128)(2,1)} %copy.94) | data formatting | bytes 6553600 | tf_op jit(solution)/shard_map/while/body/reshape | solution.py:61
  171.1 1.6 convolution_convert_fusion.8
  172.7 2.6 convolution_add_fusion.2
  175.3 0.2 fusion.110
  175.8 1.3 convolution_convert_fusion.7
  177.2 0.2 reshape.453
  177.6 1.9 gather_fusion
  179.5 0.3 copy.95
  179.9 2.1 fusion.107
  182.0 2.1 fusion.108
  184.1 6.4 %copy.94 = bf16[8,20,16,5,128]{4,3,2,1,0:T(8,128)(2,1)} copy(bf16[8,20,16,5,128]{4,2,1,3,0:T(8,128)(2,1)S(1)} %fusion.108) | data formatting | bytes 6553600 | tf_op jit(solution)/shard_map/while/body/convert_element_type | solution.py:61
  190.4 7.0 %reshape.454 = bf16[8,320,640]{2,1,0:T(8,128)(2,1)S(1)} reshape(bf16[8,20,16,5,128]{4,3,2,1,0:T(8,128)(2,1)} %copy.94) | data formatting | bytes 6553600 | tf_op jit(solution)/shard_map/while/body/reshape | solution.py:61
  197.4 1.6 convolution_convert_fusion.8
  199.0 2.6 convolution_add_fusion.2
  201.6 1.1 copy.56
  202.9 3.4 %collective-permute-start = (f32[20,640]{1,0:T(8,128)S(1)}, f32[20,640]{1,0:T(8,128)S(1)}, u32[]{:S(2)}, u32[]{:S(2)}) collective-permute-start(f32[20,640]{1,0:T(8,128)S(1)} %slice.238), channel_id=1, source_target_pairs={{1,0},{2,1},{3,2},{4,3},{5,4},{6,5},{7,6},{9,8},{10,9},{11,10},{12... | collective-permute-start | bytes 153608 | tf_op jit(solution)/shard_map/ppermute | solution.py:15
  206.2 2.7 collective-permute-done
  209.0 4.3 %collective-permute-start.1 = (f32[20,640]{1,0:T(8,128)S(1)}, f32[20,640]{1,0:T(8,128)S(1)}, u32[]{:S(2)}, u32[]{:S(2)}) collective-permute-start(f32[20,640]{1,0:T(8,128)S(1)} %get-tuple-element.318), channel_id=1, source_target_pairs={{0,1},{1,2},{2,3},{3,4},{4,5},{5,6},{6,7},{8,9},{9,10},{10,11},{11... | collective-permute-start | bytes 153608 | tf_op jit(solution)/shard_map/ppermute | solution.py:15
  213.3 0.6 compare_reduce_fusion.1
  214.0 0.4 scatter-add.34
  214.4 1.7 collective-permute-done.1
  216.0 0.6 scatter-add.35
  216.7 52.4 %collective-permute-start.2 = (f32[64,128]{1,0:T(8,128)S(1)}, f32[64,128]{1,0:T(8,128)S(1)}, u32[]{:S(2)}, u32[]{:S(2)}) collective-permute-start(f32[64,128]{1,0:T(8,128)S(1)} %get-tuple-element.317), channel_id=1, source_target_pairs={{8,0},{16,8},{24,16},{9,1},{17,9},{25,17},{10,2},{18,10},{26,18},{... | collective-permute-start | bytes 98312 | tf_op jit(solution)/shard_map/ppermute | solution.py:15
  269.1 1.4 fusion.39
  270.6 0.7 copy.63
  271.4 1.9 collective-permute-start.3
  273.3 0.5 scatter-add.36
  273.8 3.7 %collective-permute-done.3 = f32[64,128]{1,0:T(8,128)S(1)} collective-permute-done((f32[64,128]{1,0:T(8,128)S(1)}, f32[64,128]{1,0:T(8,128)S(1)}, u32[]{:S(2)}, u32[]{:S(2)}) %collective-permute-start.3) | collective-permute-done | bytes 32800 | tf_op jit(solution)/shard_map/ppermute | solution.py:15
  277.5 0.7 add_select_fusion
  278.2 0.4 scatter-add.39
  278.7 0.6 copy-done.1
  (60 shorter events, 2.1 us)
Async XLA Ops:
  0.6 138.1 %copy-start = (f32[64,20]{0,1:T(8,128)S(1)}, f32[64,20]{0,1:T(8,128)}, u32[]{:S(2)}) copy-start(f32[64,20]{0,1:T(8,128)} %param.35) | copy-start | bytes 15364
  0.6 14.1 %copy-start.2 = (f32[20,41]{1,0:T(8,128)S(1)}, f32[20,41]{1,0:T(8,128)}, u32[]{:S(2)}) copy-start(f32[20,41]{1,0:T(8,128)} %param.36) | copy-start | bytes 9844
  0.7 14.2 %copy-start.3 = (f32[20,41]{1,0:T(8,128)S(1)}, f32[20,41]{1,0:T(8,128)}, u32[]{:S(2)}) copy-start(f32[20,41]{1,0:T(8,128)} %param.37) | copy-start | bytes 9844
  4.9 136.3 %all-to-all-start = ((bf16[32,16,512]{2,1,0:T(8,128)(2,1)}), bf16[32,16,512]{2,1,0:T(8,128)(2,1)S(1)}, u32[]{:S(2)}, u32[]{:S(2)}) async-start(bf16[32,16,512]{2,1,0:T(8,128)(2,1)} %copy.50), calls=%async_computation | async-start | bytes 1048576 | tf_op jit(solution)/shard_map/all_to_all | solution.py:70
  77.4 61.4 %copy-start.4 = (s32[32]{0:T(128)S(1)}, s32[32]{0:T(128)}, u32[]{:S(2)}) copy-start(s32[32]{0:T(128)} %param.34) | copy-start | bytes 388
  141.2 128.0 %all-to-all-start.1 = ((bf16[32,16,512]{2,1,0:T(8,128)(2,1)}), bf16[32,16,512]{2,1,0:T(8,128)(2,1)}, u32[]{:S(2)}, u32[]{:S(2)}) async-start(bf16[32,16,512]{2,1,0:T(8,128)(2,1)} %copy.61), calls=%async_computation.1 | async-start | bytes 1048576 | tf_op jit(solution)/shard_map/all_to_all | solution.py:71
  202.9 6.1 %collective-permute-start = (f32[20,640]{1,0:T(8,128)S(1)}, f32[20,640]{1,0:T(8,128)S(1)}, u32[]{:S(2)}, u32[]{:S(2)}) collective-permute-start(f32[20,640]{1,0:T(8,128)S(1)} %slice.238), channel_id=1, source_target_pairs={{1,0},{2,1},{3,2},{4,3},{5,4},{6,5},{7,6},{9,8},{10,9},{11,10},{12... | collective-permute-start | bytes 153608 | tf_op jit(solution)/shard_map/ppermute | solution.py:15
  209.0 7.0 %collective-permute-start.1 = (f32[20,640]{1,0:T(8,128)S(1)}, f32[20,640]{1,0:T(8,128)S(1)}, u32[]{:S(2)}, u32[]{:S(2)}) collective-permute-start(f32[20,640]{1,0:T(8,128)S(1)} %get-tuple-element.318), channel_id=1, source_target_pairs={{0,1},{1,2},{2,3},{3,4},{4,5},{5,6},{6,7},{8,9},{9,10},{10,11},{11... | collective-permute-start | bytes 153608 | tf_op jit(solution)/shard_map/ppermute | solution.py:15
  216.7 56.6 %collective-permute-start.2 = (f32[64,128]{1,0:T(8,128)S(1)}, f32[64,128]{1,0:T(8,128)S(1)}, u32[]{:S(2)}, u32[]{:S(2)}) collective-permute-start(f32[64,128]{1,0:T(8,128)S(1)} %get-tuple-element.317), channel_id=1, source_target_pairs={{8,0},{16,8},{24,16},{9,1},{17,9},{25,17},{10,2},{18,10},{26,18},{... | collective-permute-start | bytes 98312 | tf_op jit(solution)/shard_map/ppermute | solution.py:15
  271.4 6.2 %collective-permute-start.3 = (f32[64,128]{1,0:T(8,128)S(1)}, f32[64,128]{1,0:T(8,128)S(1)}, u32[]{:S(2)}, u32[]{:S(2)}) collective-permute-start(f32[64,128]{1,0:T(8,128)S(1)} %get-tuple-element.316), channel_id=1, source_target_pairs={{0,8},{8,16},{16,24},{1,9},{9,17},{17,25},{2,10},{10,18},{18,26},{... | collective-permute-start | bytes 98312 | tf_op jit(solution)/shard_map/ppermute | solution.py:15
  278.7 0.7 copy-start.1
where the time goes:
time: 282 us; the launch traced here: 279 us
  local copies, waits for them, and re-layouts  166 us (59%)
  starting transfers between devices  73.8 us (26%)
  matrix products  22.2 us (8%)
  waiting for transfers between devices  8.16 us (3%)
  other arithmetic  7.57 us (3%)
    ppermute x4, starting transfers between devices, from_behind(): lax.ppermute(value, axis, [(source, source + steps) for source in range(i...  62 us
    gather x2, local copies, waits for them, and re-layouts, band_pair(): jnp.take(basis_across, jnp.clip(offset_prev, 0, 2 * margin), axis=1)  61.4 us
    gather x2, local copies, waits for them, and re-layouts, band_pair(): jnp.take(basis_across, jnp.clip(offset_now, 0, 2 * margin), axis=1)  61.3 us
    reshape x2, local copies, waits for them, and re-layouts, convolve(): swept_rows.astype(jnp.bfloat16).reshape(block_count, -1, out_width)  13.9 us
    convert_element_type x2, local copies, waits for them, and re-layouts, convolve(): swept_rows.astype(jnp.bfloat16).reshape(block_count, -1, out_width)  12.7 us
    ppermute x4, waiting for transfers between devices, from_behind(): lax.ppermute(value, axis, [(source, source + steps) for source in range(i...  8.16 us
    all_to_all x1, starting transfers between devices, deliver(): lax.all_to_all(first_plane, ('skyx', 'skyy'), split_axis=0, concat_axis=0...  5.89 us
    all_to_all x1, starting transfers between devices, deliver(): lax.all_to_all(second_plane, ('skyx', 'skyy'), split_axis=0, concat_axis=...  5.89 us
  transfers between devices with their start and end apart: 6, of which 3 were waited for; matrix products, arithmetic and copies ran while one was open for 68% of the time, Pallas kernels for 0%

commit v1 on v0

v1 whole, which is shorter than its diff:
```python
import functools

import jax
import jax.numpy as jnp
from jax import lax
from jax.experimental import pallas as pl
from jax.experimental.pallas import tpu as pltpu
from jax.sharding import PartitionSpec as P

RS = 4
LANES = 128
LEAD = 4
GROUP = 4
MESH = pl.DeviceIdType.MESH


def kernel(
    nx,
    ny,
    taps,
    pick_ref,
    image_ref,
    ivar_ref,
    code_ref,
    coef_ref,
    table_ref,
    across_ref,
    down_ref,
    coadd_ref,
    weight_ref,
    send,
    recv,
    across_pad,
    down_pad,
    coef_rows,
    chosen,
    bands,
    mixer,
    total,
    ext,
    edge_rows,
    edge_cols,
    edge_corners,
    send_sem,
    recv_sem,
    edge_send_sem,
    edge_recv_sem,
):
    count = nx * ny
    _, rows, width = image_ref.shape
    patch_rows = RS * rows
    channels = across_ref.shape[0]
    margin = (taps - 1) // 2
    tall = ext.shape[0]
    tiles = width // LANES
    spill = margin + LEAD
    mx = lax.axis_index("skyx")
    my = lax.axis_index("skyy")
    me = mx * ny + my

    def partner(step):
        tx = lax.rem(mx + step // ny, nx)
        ty = lax.rem(my + lax.rem(step, ny), ny)
        return tx, ty

    barrier = pltpu.get_barrier_semaphore()

    def greet(step, carry):
        tx, ty = partner(step)
        pl.semaphore_signal(barrier, inc=1, device_id=(tx, ty), device_id_type=MESH)
        return carry

    lax.fori_loop(1, count, greet, 0)

    def stage(patch, carry):
        block = pick_ref[patch]
        weight = ivar_ref[block].astype(jnp.float32)
        send[0, patch] = (weight * image_ref[block].astype(jnp.float32)).astype(jnp.bfloat16)
        send[1, patch] = ivar_ref[block]
        return carry

    lax.fori_loop(0, count, stage, 0)
    recv[0, me] = send[0, me]
    recv[1, me] = send[1, me]
    pl.semaphore_wait(barrier, count - 1)

    def block_copy(plane, target, source, device):
        return pltpu.make_async_remote_copy(
            src_ref=send.at[plane, target],
            dst_ref=recv.at[plane, source],
            send_sem=send_sem.at[plane, target],
            recv_sem=recv_sem.at[plane, source],
            device_id=device,
            device_id_type=MESH,
        )

    for plane in range(2):

        def start(step, carry):
            tx, ty = partner(step)
            block_copy(plane, tx * ny + ty, me, (tx, ty)).start()
            return carry

        lax.fori_loop(1, count, start, 0)

    across_pad[...] = jnp.zeros_like(across_pad)
    across_pad[:, :taps] = across_ref[...]
    down_pad[...] = jnp.zeros_like(down_pad)
    down_pad[:, :taps] = down_ref[...]
    down_pad[...] = pltpu.roll(down_pad[...], LEAD, 1)
    code = code_ref[...]
    place = lax.broadcasted_iota(jnp.int32, (patch_rows, code.shape[1]), 0)
    chosen_rows = (place == code).astype(jnp.float32).astype(jnp.bfloat16)
    chosen[:patch_rows] = chosen_rows
    chosen[patch_rows:] = chosen_rows
    sets = lax.broadcasted_iota(jnp.int32, (table_ref.shape[0], code.shape[1]), 0)
    coef_rows[...] = lax.dot_general(
        table_ref[...],
        (sets == coef_ref[...]).astype(jnp.float32),
        (((0,), (0,)), ((), ())),
        precision=lax.Precision.HIGHEST,
        preferred_element_type=jnp.float32,
    )

    def build(channel, carry):
        row = jnp.broadcast_to(across_pad[pl.ds(channel, 1), :], (LANES, 2 * LANES))
        band = pltpu.roll(row, 0, 1, stride=1, stride_axis=0)
        bands[channel, :LANES] = band[:, LANES:].astype(jnp.bfloat16)
        bands[channel, LANES:] = band[:, :LANES].astype(jnp.bfloat16)
        row = jnp.broadcast_to(down_pad[pl.ds(channel, 1), :], (patch_rows, LANES))
        shifted = pltpu.roll(row, 0, 1, stride=1, stride_axis=0)
        high = shifted.astype(jnp.bfloat16)
        low = (shifted - high.astype(jnp.float32)).astype(jnp.bfloat16)
        picked = lax.dot_general(
            jnp.concatenate([high, low], axis=0),
            chosen[...],
            (((0,), (0,)), ((), ())),
            preferred_element_type=jnp.float32,
        )
        mixed = picked[:tall] * coef_rows[pl.ds(channel, 1), :]
        start_row = pl.multiple_of(channel * tall, 16)
        mixer[pl.ds(start_row, tall), :] = mixed.astype(jnp.bfloat16)
        return carry

    lax.fori_loop(0, channels, build, 0)
    total[...] = jnp.zeros_like(total)

    def arrive(plane):
        def wait(step, carry):
            tx, ty = partner(step)
            block_copy(plane, me, tx * ny + ty, (tx, ty)).wait_recv()
            return carry

        lax.fori_loop(1, count, wait, 0)

    arrive(0)
    planes = recv[0].reshape(count * rows, width)
    zeros = jnp.zeros((tall, LANES), jnp.bfloat16)

    def convolve(turn, carry):
        start_row = pl.multiple_of(turn * GROUP * tall, 16)
        mixed = jnp.dot(
            mixer[pl.ds(start_row, GROUP * tall), :], planes, preferred_element_type=jnp.float32
        ).astype(jnp.bfloat16)
        summed = total[...]
        for member in range(GROUP):
            own = mixed[member * tall : (member + 1) * tall]
            padded = jnp.concatenate([zeros, own, zeros], axis=1)
            pairs = jnp.concatenate(
                [padded[:, LANES * t : LANES * (t + 2)] for t in range(tiles + 1)], axis=0
            )
            summed = summed + jnp.dot(
                pairs, bands[turn * GROUP + member], preferred_element_type=jnp.float32
            )
        total[...] = summed
        return carry

    lax.fori_loop(0, channels // GROUP, convolve, 0)
    joined = jnp.concatenate([total[t * tall : (t + 1) * tall] for t in range(tiles + 1)], axis=1)
    ext[...] = pltpu.roll(joined, width + LANES - margin, 1)

    top, middle, bottom = pl.ds(0, spill), pl.ds(spill, patch_rows), pl.ds(spill + patch_rows, spill)
    side, body_cols = pl.ds(width, LANES), pl.ds(0, width)
    plan = [
        (0, -1, (top, body_cols), edge_rows.at[1]),
        (0, 1, (bottom, body_cols), edge_rows.at[0]),
        (-1, 0, (middle, side), edge_cols.at[1]),
        (1, 0, (middle, side), edge_cols.at[0]),
        (-1, -1, (top, side), edge_corners.at[3]),
        (1, -1, (top, side), edge_corners.at[2]),
        (-1, 1, (bottom, side), edge_corners.at[1]),
        (1, 1, (bottom, side), edge_corners.at[0]),
    ]

    def exists(dx, dy):
        return (mx + dx >= 0) & (mx + dx < nx) & (my + dy >= 0) & (my + dy < ny)

    def edge_copy(number):
        dx, dy, piece, landing = plan[number]
        return pltpu.make_async_remote_copy(
            src_ref=ext.at[piece],
            dst_ref=landing,
            send_sem=edge_send_sem.at[number],
            recv_sem=edge_recv_sem.at[number],
            device_id=(mx + dx, my + dy),
            device_id_type=MESH,
        )

    for number, (dx, dy, _, _) in enumerate(plan):

        @pl.when(exists(dx, dy))
        def _():
            edge_copy(number).start()

    coadd_ref[...] = ext[middle, body_cols]

    arrive(1)
    weight_ref[...] = jnp.dot(
        chosen_rows_of(chosen, patch_rows),
        recv[1].reshape(count * rows, width),
        preferred_element_type=jnp.float32,
    )

    lane = lax.broadcasted_iota(jnp.int32, (spill, LANES), 1)
    lane_tall = lax.broadcasted_iota(jnp.int32, (patch_rows, LANES), 1)
    low_rows, high_rows = pl.ds(0, spill), pl.ds(patch_rows - spill, spill)
    left, right = pl.ds(0, LANES), pl.ds(width - LANES, LANES)

    def from_side(value, lanes, dx):
        if dx < 0:
            return jnp.where(lanes < margin, value, 0.0)
        return jnp.where(lanes >= LANES - margin, value, 0.0)

    for number, (dx, dy, _, landing) in enumerate(plan):
        @pl.when(exists(-dx, -dy))
        def _():
            edge_copy(number).wait_recv()
            if dx == 0:
                here = low_rows if dy > 0 else high_rows
                coadd_ref[here, :] += landing[...]
            elif dy == 0:
                here = left if dx > 0 else right
                coadd_ref[:, here] += from_side(landing[...], lane_tall, -dx)
            else:
                here = (low_rows if dy > 0 else high_rows, left if dx > 0 else right)
                coadd_ref[here] += from_side(landing[...], lane, -dx)

    for plane in range(2):

        def sent(step, carry):
            tx, ty = partner(step)
            block_copy(plane, tx * ny + ty, me, (tx, ty)).wait_send()
            return carry

        lax.fori_loop(1, count, sent, 0)
    for number, (dx, dy, _, _) in enumerate(plan):

        @pl.when(exists(dx, dy))
        def _():
            edge_copy(number).wait_send()


def chosen_rows_of(chosen, patch_rows):
    return chosen[:patch_rows]


def body(
    image, inverse_var, patch_of, row_of, valid, coef_index, coef_table, basis_across, basis_down
):
    nx, ny = lax.axis_size("skyx"), lax.axis_size("skyy")
    count = nx * ny
    blocks, rows, width = image.shape
    channels, taps = basis_across.shape
    margin = (taps - 1) // 2
    patch_rows = RS * rows
    spill = margin + LEAD
    tall = patch_rows + 2 * spill
    tiles = width // LANES
    me = lax.axis_index("skyx") * ny + lax.axis_index("skyy")
    targets = patch_of[:, 0].reshape(count, blocks)
    mine = lax.dynamic_slice_in_dim(targets, me, 1)
    patches = jnp.arange(count, dtype=jnp.int32)[:, None]
    slots = jnp.arange(blocks, dtype=jnp.int32)[None, :]
    pick = jnp.sum(jnp.where(mine == patches, slots, 0), axis=1)
    usable = (targets == me) & (valid.reshape(count, blocks) > 0)
    far = 1 << 20
    first = jnp.sum(jnp.where(usable, row_of.reshape(count, blocks) * rows + far, 0), axis=1) - far
    code = (first[:, None] + jnp.arange(rows, dtype=jnp.int32)[None, :]).reshape(1, count * rows)
    sets = jnp.broadcast_to(coef_index[:, None], (count, rows)).reshape(1, count * rows)

    vmem = pl.BlockSpec(memory_space=pltpu.VMEM)
    smem = pl.BlockSpec(memory_space=pltpu.SMEM)
    deep = count * rows
    return pl.pallas_call(
        functools.partial(kernel, nx, ny, taps),
        out_shape=(
            jax.ShapeDtypeStruct((patch_rows, width), jnp.float32),
            jax.ShapeDtypeStruct((patch_rows, width), jnp.float32),
        ),
        in_specs=[smem] + [vmem] * 7,
        out_specs=(vmem, vmem),
        scratch_shapes=[
            pltpu.VMEM((2, count, rows, width), jnp.bfloat16),
            pltpu.VMEM((2, count, rows, width), jnp.bfloat16),
            pltpu.VMEM((channels, 2 * LANES), jnp.float32),
            pltpu.VMEM((channels, LANES), jnp.float32),
            pltpu.VMEM((channels, deep), jnp.float32),
            pltpu.VMEM((2 * patch_rows, deep), jnp.bfloat16),
            pltpu.VMEM((channels, 2 * LANES, LANES), jnp.bfloat16),
            pltpu.VMEM((channels * tall, deep), jnp.bfloat16),
            pltpu.VMEM(((tiles + 1) * tall, LANES), jnp.float32),
            pltpu.VMEM((tall, width + LANES), jnp.float32),
            pltpu.VMEM((2, spill, width), jnp.float32),
            pltpu.VMEM((2, patch_rows, LANES), jnp.float32),
            pltpu.VMEM((4, spill, LANES), jnp.float32),
            pltpu.SemaphoreType.DMA((2, count)),
            pltpu.SemaphoreType.DMA((2, count)),
            pltpu.SemaphoreType.DMA((8,)),
            pltpu.SemaphoreType.DMA((8,)),
        ],
        compiler_params=pltpu.CompilerParams(
            collective_id=0, has_side_effects=True, vmem_limit_bytes=48 * 1024 * 1024
        ),
    )(pick, image, inverse_var, code, sets, coef_table, basis_across, basis_down)


def solution(mesh):
    placed = (
        P(("skyx", "skyy"), None, None),
        P(("skyx", "skyy"), None, None),
        P(),
        P(),
        P(),
        P(),
        P(),
        P(),
        P(),
    )
    return jax.shard_map(
        body,
        mesh=mesh,
        in_specs=placed,
        out_specs=(P("skyy", "skyx"), P("skyy", "skyx")),
        check_vma=False,
    )
```

time: 282 us -> 44.4 us (0.16)
  the two profiles are of different devices: /device:TPU:20 before, /device:TPU:0 now
where the time goes in v1:
time: 44.4 us; the launch traced here: 43.7 us
  Pallas kernels  35.1 us (79%)
  local copies, waits for them, and re-layouts  6.98 us (16%)
  other arithmetic  1 us (2%)
  between operations  0.7 us (2%)
    pallas_call x1, Pallas kernels, body(): pl.pallas_call(functools.partial(kernel, nx, ny, taps), out_shape=(jax.Sh...  35.1 us
    unnamed x22, local copies, waits for them, and re-layouts  6.5 us

profile of v1, /device:TPU:0, one launch (start us, length us, event | category | flops | bytes accessed | tf_op | source)
XLA Modules:
  0.0 43.7 jit_solution(10561285426618475702)
XLA Ops:
  0.6 0.0 copy-start.5
  0.6 0.7 %copy-done.5 = s32[512]{0:T(512)S(1)} copy-done((s32[512]{0:T(512)S(1)}, s32[512]{0:T(512)}, u32[]{:S(2)}) %copy-start.5) | copy-done | bytes 2072
  1.3 0.0 copy-start.6
  1.3 0.5 %broadcast.43 = s32[]{:T(128)} broadcast(s32[]{:T(128)} %constant.5.clone.1), dimensions={} | broadcast | bytes 8 | tf_op args[2]
  1.8 0.2 copy-done.6
  2.0 0.0 copy-start.7
  2.0 0.7 %reduce.3 = s32[512]{0:T(512)S(1)} reduce(s32[512,1]{0,1:T(1,128)S(1)} %copy-done.6, s32[]{:T(128)} %broadcast.43), dimensions={1}, to_apply=%param.11.reduce_sub_computation.3 | reduce | bytes 4100 | tf_op args[2]
  2.7 0.0 copy-done.7
  2.7 0.1 gt.12
  2.8 0.1 reshape_squeeze.3
  2.9 0.1 select_reduce_fusion.1.pick_ref
  3.0 0.1 add.49
  3.1 0.1 select_reduce_fusion
  3.2 0.1 iota_add_fusion
  3.3 0.0 copy-start.8
  3.3 0.1 add.52.code_ref
  3.4 0.6 %copy-done.8 = s32[32]{0:T(128)S(1)} copy-done((s32[32]{0:T(128)S(1)}, s32[32]{0:T(128)}, u32[]{:S(2)}) %copy-start.8) | copy-done | bytes 152
  3.9 0.1 broadcast_in_dim.32
  4.0 0.0 copy-start.4
  4.0 0.1 reshape.50.coef_ref
  4.1 0.6 %copy-done.4 = f32[64,20]{0,1:T(8,128)S(1)} copy-done((f32[64,20]{0,1:T(8,128)S(1)}, f32[64,20]{0,1:T(8,128)}, u32[]{:S(2)}) %copy-start.4) | copy-done | bytes 5144
  4.7 0.0 copy-start.2
  4.7 0.0 copy-start.3
  4.7 0.1 copy.12.table_ref
  4.8 0.6 %copy-done.2 = f32[20,41]{1,0:T(8,128)S(1)} copy-done((f32[20,41]{1,0:T(8,128)S(1)}, f32[20,41]{1,0:T(8,128)}, u32[]{:S(2)}) %copy-start.2) | copy-done | bytes 3304
  5.4 0.0 copy-done.3
  5.4 0.0 copy-start
  5.5 0.9 %copy-done = bf16[16,16,512]{2,1,0:T(8,128)(2,1)S(1)} copy-done((bf16[16,16,512]{2,1,0:T(8,128)(2,1)S(1)}, bf16[16,16,512]{2,1,0:T(8,128)(2,1)}, u32[]{:S(2)}) %copy-start) | copy-done | bytes 262168
  6.4 0.0 copy-start.1
  6.4 0.9 %copy-done.1 = bf16[16,16,512]{2,1,0:T(8,128)(2,1)S(1)} copy-done((bf16[16,16,512]{2,1,0:T(8,128)(2,1)S(1)}, bf16[16,16,512]{2,1,0:T(8,128)(2,1)}, u32[]{:S(2)}) %copy-start.1) | copy-done | bytes 262168
  7.3 35.1 %shard_map.104 = (f32[64,512]{1,0:T(8,128)S(1)}, f32[64,512]{1,0:T(8,128)S(1)}) custom-call(s32[32]{0:T(128)S(1)} %select_reduce_fusion.1.pick_ref, bf16[16,16,512]{2,1,0:T(8,128)(2,1)S(1)} %copy-done, bf16[16,16,512]{2,1,0:T(8,128)(2,1)S(1)} %copy-done.1, s32[1,512]{1,0:T(1,128)S(1)} %add.52.code_ref, s32[1,512]{1,0:T(1,128)S(1)} %reshape.50.coef_ref, ...), custom_call_target="tpu_custom_call" | custom-call | tf_op jit(solution)/shard_map/pallas_call | solution.py:294
  42.4 0.7 %copy.15 = f32[64,512]{1,0:T(8,128)} copy(f32[64,512]{1,0:T(8,128)S(1)} %get-tuple-element.4) | data formatting | bytes 262144
  43.1 0.7 %copy.16 = f32[64,512]{1,0:T(8,128)} copy(f32[64,512]{1,0:T(8,128)S(1)} %get-tuple-element.5) | data formatting | bytes 262144
  (4 shorter events, 0.0 us)
Async XLA Ops:
  0.6 0.7 %copy-start.5 = (s32[512]{0:T(512)S(1)}, s32[512]{0:T(512)}, u32[]{:S(2)}) copy-start(s32[512]{0:T(512)} %param.13) | copy-start | bytes 6148
  1.3 0.7 %copy-start.6 = (s32[512,1]{0,1:T(1,128)S(1)}, s32[512,1]{0,1:T(1,128)}, u32[]{:S(2)}) copy-start(s32[512,1]{0,1:T(1,128)} %param.11) | copy-start | bytes 6148
  2.0 0.7 %copy-start.7 = (s32[512]{0:T(512)S(1)}, s32[512]{0:T(512)}, u32[]{:S(2)}) copy-start(s32[512]{0:T(512)} %param.12) | copy-start | bytes 6148
  3.3 0.7 %copy-start.8 = (s32[32]{0:T(128)S(1)}, s32[32]{0:T(128)}, u32[]{:S(2)}) copy-start(s32[32]{0:T(128)} %param.14) | copy-start | bytes 388
  4.0 0.7 %copy-start.4 = (f32[64,20]{0,1:T(8,128)S(1)}, f32[64,20]{0,1:T(8,128)}, u32[]{:S(2)}) copy-start(f32[64,20]{0,1:T(8,128)} %param.15) | copy-start | bytes 15364
  4.7 0.7 %copy-start.2 = (f32[20,41]{1,0:T(8,128)S(1)}, f32[20,41]{1,0:T(8,128)}, u32[]{:S(2)}) copy-start(f32[20,41]{1,0:T(8,128)} %across_ref.1) | copy-start | bytes 9844
  4.7 0.7 %copy-start.3 = (f32[20,41]{1,0:T(8,128)S(1)}, f32[20,41]{1,0:T(8,128)}, u32[]{:S(2)}) copy-start(f32[20,41]{1,0:T(8,128)} %down_ref.1) | copy-start | bytes 9844
  5.4 0.9 %copy-start = (bf16[16,16,512]{2,1,0:T(8,128)(2,1)S(1)}, bf16[16,16,512]{2,1,0:T(8,128)(2,1)}, u32[]{:S(2)}) copy-start(bf16[16,16,512]{2,1,0:T(8,128)(2,1)} %image_ref.1) | copy-start | bytes 786436
  6.4 0.9 %copy-start.1 = (bf16[16,16,512]{2,1,0:T(8,128)(2,1)S(1)}, bf16[16,16,512]{2,1,0:T(8,128)(2,1)}, u32[]{:S(2)}) copy-start(bf16[16,16,512]{2,1,0:T(8,128)(2,1)} %ivar_ref.1) | copy-start | bytes 786436

commit v2 on v1

v2 whole, which is shorter than its diff:
```python
import functools

import jax
import jax.numpy as jnp
from jax import lax
from jax.experimental import pallas as pl
from jax.experimental.pallas import tpu as pltpu
from jax.sharding import PartitionSpec as P

RS = 4
LANES = 128
LEAD = 4
INNER = 2
GROUP = 4
MESH = pl.DeviceIdType.MESH


def kernel(
    nx,
    ny,
    taps,
    image_hbm,
    ivar_hbm,
    patch_hbm,
    row_hbm,
    valid_hbm,
    sets_hbm,
    table_hbm,
    across_hbm,
    down_hbm,
    coadd_ref,
    weight_ref,
    image_ref,
    ivar_ref,
    patch_scalars,
    patch_lanes,
    row_lanes,
    valid_lanes,
    sets_lanes,
    table_ref,
    across_ref,
    down_ref,
    send,
    recv,
    keep_send,
    keep_recv,
    part_send,
    part_recv,
    across_pad,
    down_pad,
    coef_rows,
    chosen,
    bands,
    mixer,
    mixed_tiles,
    ext,
    edge_rows,
    edge_cols,
    edge_corners,
    load_sem,
    send_sem,
    recv_sem,
    keep_send_sem,
    keep_recv_sem,
    part_send_sem,
    part_recv_sem,
    edge_send_sem,
    edge_recv_sem,
):
    count = nx * ny
    planes = ny // INNER
    members = nx * INNER
    blocks, rows, width = image_ref.shape
    patch_rows = RS * rows
    channels = across_ref.shape[0]
    margin = (taps - 1) // 2
    tall = ext.shape[0]
    tiles = width // LANES
    spill = margin + LEAD
    mx = lax.axis_index("skyx")
    my = lax.axis_index("skyy")
    me = mx * ny + my
    hi, lo = my // INNER, lax.rem(my, INNER)

    def partner(step):
        back = count - 1 - step
        tx = lax.rem(mx + lax.rem(back // INNER, nx), nx)
        thi = lax.rem(hi + back // members, planes)
        tlo = lax.rem(lo + lax.rem(back, INNER), INNER)
        return tx, thi, tlo

    barrier = pltpu.get_barrier_semaphore()
    pairs = [
        (patch_hbm, patch_scalars),
        (image_hbm, image_ref),
        (ivar_hbm, ivar_ref),
        (patch_hbm, patch_lanes),
        (row_hbm, row_lanes),
        (valid_hbm, valid_lanes),
        (sets_hbm, sets_lanes),
        (table_hbm, table_ref),
        (across_hbm, across_ref),
        (down_hbm, down_ref),
    ]
    loads = [
        pltpu.make_async_copy(source, landing, load_sem.at[number])
        for number, (source, landing) in enumerate(pairs)
    ]
    for load in loads:
        load.start()

    def greet(step, carry):
        tx, thi, tlo = partner(step)
        pl.semaphore_signal(
            barrier, inc=1, device_id=(tx, thi * INNER + tlo), device_id_type=MESH
        )
        return carry

    lax.fori_loop(0, count - 1, greet, 0)
    for load in loads[:3]:
        load.wait()
    targets = [patch_scalars[0, me * blocks + k] for k in range(blocks)]

    def stage(tx, thi, tlo):
        patch = tx * ny + thi * INNER + tlo
        block = 0
        for k in range(1, blocks):
            block = jnp.where(targets[k] == patch, k, block)
        weight = ivar_ref[block]
        product = weight.astype(jnp.float32) * image_ref[block].astype(jnp.float32)
        send[patch] = product.astype(jnp.bfloat16)
        keep_send[tx * INNER + tlo, thi] = weight
        return patch

    def block_copy(target, source, device):
        return pltpu.make_async_remote_copy(
            src_ref=send.at[target],
            dst_ref=recv.at[source],
            send_sem=send_sem.at[target],
            recv_sem=recv_sem.at[source],
            device_id=device,
            device_id_type=MESH,
        )

    def keep_copy(target, source, device):
        return pltpu.make_async_remote_copy(
            src_ref=keep_send.at[target],
            dst_ref=keep_recv.at[source],
            send_sem=keep_send_sem.at[target],
            recv_sem=keep_recv_sem.at[source],
            device_id=device,
            device_id_type=MESH,
        )

    def part_copy(target, source, device):
        return pltpu.make_async_remote_copy(
            src_ref=part_send.at[target],
            dst_ref=part_recv.at[source],
            send_sem=part_send_sem.at[target],
            recv_sem=part_recv_sem.at[source],
            device_id=device,
            device_id_type=MESH,
        )

    pl.semaphore_wait(barrier, count - 1)

    def start(step, carry):
        tx, thi, tlo = partner(step)
        patch = stage(tx, thi, tlo)
        block_copy(patch, me, (tx, thi * INNER + tlo)).start()
        return carry

    lax.fori_loop(0, count - 1, start, 0)
    stage(mx, hi, lo)
    recv[me] = send[me]

    def member_of(step):
        return lax.rem(mx + step // INNER, nx), lax.rem(lo + lax.rem(step, INNER), INNER)

    own_member = mx * INNER + lo

    def start_keep(step, carry):
        tx, tlo = member_of(step)
        keep_copy(tx * INNER + tlo, own_member, (tx, hi * INNER + tlo)).start()
        return carry

    lax.fori_loop(1, members, start_keep, 0)
    keep_recv[own_member] = keep_send[own_member]
    for load in loads[3:]:
        load.wait()

    across_pad[...] = jnp.zeros_like(across_pad)
    across_pad[:, :taps] = across_ref[...]
    down_pad[...] = jnp.zeros_like(down_pad)
    down_pad[:, :taps] = down_ref[...]
    down_pad[...] = pltpu.roll(down_pad[...], LEAD, 1)

    def same(condition):
        return condition.astype(jnp.float32).astype(jnp.bfloat16)

    def iota(shape, dim):
        return lax.broadcasted_iota(jnp.int32, shape, dim)

    def spread(slots, groups):
        lanes = slots.shape[1]
        tall_flags = jnp.concatenate(
            [jnp.broadcast_to(slots[s : s + 1], (rows, lanes)) for s in range(groups * RS)], axis=0
        )
        shape = tall_flags.shape
        keep = lax.rem(iota(shape, 0), rows) == lax.rem(iota(shape, 1), rows)
        return jnp.where(keep, tall_flags, 0.0).astype(jnp.bfloat16)

    spot = jnp.where(valid_lanes[...] > 0, patch_lanes[...] * RS + row_lanes[...], -1)
    wide = count * blocks
    own_slots = same(iota((8, wide), 0) + me * RS == spot)
    own_slots = jnp.where(iota((8, wide), 0) < RS, own_slots, jnp.bfloat16(0))
    chunk = LANES // rows
    repeat = same(
        iota((chunk * blocks, LANES), 0) // blocks == iota((chunk * blocks, LANES), 1) // rows
    )
    own_flags = jnp.concatenate(
        [
            jnp.dot(
                own_slots[:, g * chunk * blocks : (g + 1) * chunk * blocks],
                repeat,
                preferred_element_type=jnp.float32,
            )
            for g in range(count // chunk)
        ],
        axis=1,
    )
    own_rows = spread(own_flags, 1)
    chosen[:patch_rows] = own_rows
    chosen[patch_rows:] = own_rows

    onehot = (iota((table_ref.shape[1], count), 0) == sets_lanes[...]).astype(jnp.float32)
    coeffs = jnp.dot(
        table_ref[...],
        onehot,
        precision=lax.Precision.HIGHEST,
        preferred_element_type=jnp.float32,
    )
    deep = count * rows
    coef_rows[...] = jnp.dot(
        coeffs,
        (iota((count, deep), 0) == iota((count, deep), 1) // rows).astype(jnp.float32),
        precision=lax.Precision.HIGHEST,
        preferred_element_type=jnp.float32,
    )

    shape = (planes * RS, wide)
    wanted = (mx * ny + (iota(shape, 0) // RS) * INNER + lo) * RS + lax.rem(iota(shape, 0), RS)
    shape = (wide, members * rows)
    member = iota(shape, 1) // rows
    exposure = (member // INNER) * ny + hi * INNER + lax.rem(member, INNER)
    plane_flags = jnp.dot(
        same(wanted == spot),
        same(iota(shape, 0) // blocks == exposure),
        preferred_element_type=jnp.float32,
    )
    plane_rows = spread(plane_flags, planes)

    def build(channel, carry):
        row = jnp.broadcast_to(across_pad[pl.ds(channel, 1), :], (LANES, 2 * LANES))
        band = pltpu.roll(row, 0, 1, stride=1, stride_axis=0)
        bands[pl.ds(pl.multiple_of(channel * LANES, LANES), LANES), :] = band.astype(jnp.bfloat16)
        row = jnp.broadcast_to(down_pad[pl.ds(channel, 1), :], (patch_rows, LANES))
        shifted = pltpu.roll(row, 0, 1, stride=1, stride_axis=0)
        high = shifted.astype(jnp.bfloat16)
        low = (shifted - high.astype(jnp.float32)).astype(jnp.bfloat16)
        picked = lax.dot_general(
            jnp.concatenate([high, low], axis=0),
            chosen[...],
            (((0,), (0,)), ((), ())),
            preferred_element_type=jnp.float32,
        )
        mixed = picked[:tall] * coef_rows[pl.ds(channel, 1), :]
        start_row = pl.multiple_of(channel * tall, 16)
        mixer[pl.ds(start_row, tall), :] = mixed.astype(jnp.bfloat16)
        return carry

    lax.fori_loop(0, channels, build, 0)

    def wait_keep(step, carry):
        tx, tlo = member_of(step)
        keep_copy(own_member, tx * INNER + tlo, (tx, hi * INNER + tlo)).wait_recv()
        return carry

    lax.fori_loop(1, members, wait_keep, 0)
    for plane in range(planes):
        part_send[plane] = jnp.dot(
            plane_rows[plane * patch_rows : (plane + 1) * patch_rows],
            keep_recv[:, plane].reshape(members * rows, width),
            preferred_element_type=jnp.float32,
        ).astype(jnp.bfloat16)
    part_recv[hi] = part_send[hi]

    def wait_block(step, carry):
        tx, thi, tlo = partner(step)
        ty = thi * INNER + tlo
        block_copy(me, tx * ny + ty, (tx, ty)).wait_recv()
        return carry

    lax.fori_loop(0, count - 1, wait_block, 0)

    def plane_at(step):
        return lax.rem(hi + step, planes)

    def start_part(step, carry):
        thi = plane_at(step)
        part_copy(thi, hi, (mx, thi * INNER + lo)).start()
        return carry

    lax.fori_loop(1, planes, start_part, 0)
    arrived = recv[...].reshape(deep, width)
    for turn in range(channels // GROUP):
        mixed = jnp.dot(
            mixer[turn * GROUP * tall : (turn + 1) * GROUP * tall],
            arrived,
            preferred_element_type=jnp.float32,
        ).astype(jnp.bfloat16)
        for member in range(GROUP):
            channel = turn * GROUP + member
            for t in range(tiles):
                mixed_tiles[
                    t * tall : (t + 1) * tall, channel * LANES : (channel + 1) * LANES
                ] = mixed[member * tall : (member + 1) * tall, t * LANES : (t + 1) * LANES]
    summed = jnp.dot(mixed_tiles[...], bands[...], preferred_element_type=jnp.float32)
    zeros = jnp.zeros((tall, LANES), jnp.float32)
    now = [summed[t * tall : (t + 1) * tall, :LANES] for t in range(tiles)] + [zeros]
    after = [zeros] + [summed[t * tall : (t + 1) * tall, LANES:] for t in range(tiles)]
    joined = jnp.concatenate([a + b for a, b in zip(now, after)], axis=1)
    ext[...] = pltpu.roll(joined, width + LANES - margin, 1)

    top, middle, bottom = pl.ds(0, spill), pl.ds(spill, patch_rows), pl.ds(spill + patch_rows, spill)
    side, body_cols = pl.ds(width, LANES), pl.ds(0, width)
    plan = [
        (0, -1, (top, body_cols), edge_rows.at[1]),
        (0, 1, (bottom, body_cols), edge_rows.at[0]),
        (-1, 0, (middle, side), edge_cols.at[1]),
        (1, 0, (middle, side), edge_cols.at[0]),
        (-1, -1, (top, side), edge_corners.at[3]),
        (1, -1, (top, side), edge_corners.at[2]),
        (-1, 1, (bottom, side), edge_corners.at[1]),
        (1, 1, (bottom, side), edge_corners.at[0]),
    ]

    def exists(dx, dy):
        return (mx + dx >= 0) & (mx + dx < nx) & (my + dy >= 0) & (my + dy < ny)

    def edge_copy(number):
        dx, dy, piece, landing = plan[number]
        return pltpu.make_async_remote_copy(
            src_ref=ext.at[piece],
            dst_ref=landing,
            send_sem=edge_send_sem.at[number],
            recv_sem=edge_recv_sem.at[number],
            device_id=(mx + dx, my + dy),
            device_id_type=MESH,
        )

    for number, (dx, dy, _, _) in enumerate(plan):

        @pl.when(exists(dx, dy))
        def _():
            edge_copy(number).start()

    coadd_ref[...] = ext[middle, body_cols]

    def wait_part(step, carry):
        thi = plane_at(step)
        part_copy(hi, thi, (mx, thi * INNER + lo)).wait_recv()
        return carry

    lax.fori_loop(1, planes, wait_part, 0)
    weights = part_recv[0].astype(jnp.float32)
    for plane in range(1, planes):
        weights = weights + part_recv[plane].astype(jnp.float32)
    weight_ref[...] = weights

    lane = lax.broadcasted_iota(jnp.int32, (spill, LANES), 1)
    lane_tall = lax.broadcasted_iota(jnp.int32, (patch_rows, LANES), 1)
    low_rows, high_rows = pl.ds(0, spill), pl.ds(patch_rows - spill, spill)
    left, right = pl.ds(0, LANES), pl.ds(width - LANES, LANES)

    def from_side(value, lanes, dx):
        if dx < 0:
            return jnp.where(lanes < margin, value, 0.0)
        return jnp.where(lanes >= LANES - margin, value, 0.0)

    for number, (dx, dy, _, landing) in enumerate(plan):
        @pl.when(exists(-dx, -dy))
        def _():
            edge_copy(number).wait_recv()
            if dx == 0:
                here = low_rows if dy > 0 else high_rows
                coadd_ref[here, :] += landing[...]
            elif dy == 0:
                here = left if dx > 0 else right
                coadd_ref[:, here] += from_side(landing[...], lane_tall, -dx)
            else:
                here = (low_rows if dy > 0 else high_rows, left if dx > 0 else right)
                coadd_ref[here] += from_side(landing[...], lane, -dx)

    def sent_block(step, carry):
        tx, thi, tlo = partner(step)
        ty = thi * INNER + tlo
        block_copy(tx * ny + ty, me, (tx, ty)).wait_send()
        return carry

    def sent_keep(step, carry):
        tx, tlo = member_of(step)
        keep_copy(tx * INNER + tlo, own_member, (tx, hi * INNER + tlo)).wait_send()
        return carry

    def sent_part(step, carry):
        thi = plane_at(step)
        part_copy(thi, hi, (mx, thi * INNER + lo)).wait_send()
        return carry

    lax.fori_loop(0, count - 1, sent_block, 0)
    lax.fori_loop(1, members, sent_keep, 0)
    lax.fori_loop(1, planes, sent_part, 0)
    for number, (dx, dy, _, _) in enumerate(plan):

        @pl.when(exists(dx, dy))
        def _():
            edge_copy(number).wait_send()


def body(
    image, inverse_var, patch_of, row_of, valid, coef_index, coef_table, basis_across, basis_down
):
    nx, ny = lax.axis_size("skyx"), lax.axis_size("skyy")
    count = nx * ny
    planes, members = ny // INNER, nx * INNER
    blocks, rows, width = image.shape
    channels, taps = basis_across.shape
    margin = (taps - 1) // 2
    patch_rows = RS * rows
    spill = margin + LEAD
    tall = patch_rows + 2 * spill
    tiles = width // LANES
    deep = count * rows
    wide = count * blocks

    vmem = pl.BlockSpec(memory_space=pltpu.VMEM)
    anywhere = pl.BlockSpec(memory_space=pl.ANY)
    dma = pltpu.SemaphoreType.DMA
    return pl.pallas_call(
        functools.partial(kernel, nx, ny, taps),
        out_shape=(
            jax.ShapeDtypeStruct((patch_rows, width), jnp.float32),
            jax.ShapeDtypeStruct((patch_rows, width), jnp.float32),
        ),
        in_specs=[anywhere] * 9,
        out_specs=(vmem, vmem),
        scratch_shapes=[
            pltpu.VMEM((blocks, rows, width), jnp.bfloat16),
            pltpu.VMEM((blocks, rows, width), jnp.bfloat16),
            pltpu.SMEM((1, wide), jnp.int32),
            pltpu.VMEM((1, wide), jnp.int32),
            pltpu.VMEM((1, wide), jnp.int32),
            pltpu.VMEM((1, wide), jnp.int32),
            pltpu.VMEM((1, count), jnp.int32),
            pltpu.VMEM(coef_table.shape[::-1], jnp.float32),
            pltpu.VMEM((channels, taps), jnp.float32),
            pltpu.VMEM((channels, taps), jnp.float32),
            pltpu.VMEM((count, rows, width), jnp.bfloat16),
            pltpu.VMEM((count, rows, width), jnp.bfloat16),
            pltpu.VMEM((members, planes, rows, width), jnp.bfloat16),
            pltpu.VMEM((members, planes, rows, width), jnp.bfloat16),
            pltpu.VMEM((planes, patch_rows, width), jnp.bfloat16),
            pltpu.VMEM((planes, patch_rows, width), jnp.bfloat16),
            pltpu.VMEM((channels, 2 * LANES), jnp.float32),
            pltpu.VMEM((channels, LANES), jnp.float32),
            pltpu.VMEM((channels, deep), jnp.float32),
            pltpu.VMEM((2 * patch_rows, deep), jnp.bfloat16),
            pltpu.VMEM((channels * LANES, 2 * LANES), jnp.bfloat16),
            pltpu.VMEM((channels * tall, deep), jnp.bfloat16),
            pltpu.VMEM((tiles * tall, channels * LANES), jnp.bfloat16),
            pltpu.VMEM((tall, width + LANES), jnp.float32),
            pltpu.VMEM((2, spill, width), jnp.float32),
            pltpu.VMEM((2, patch_rows, LANES), jnp.float32),
            pltpu.VMEM((4, spill, LANES), jnp.float32),
            dma((10,)),
            dma((count,)),
            dma((count,)),
            dma((members,)),
            dma((members,)),
            dma((planes,)),
            dma((planes,)),
            dma((8,)),
            dma((8,)),
        ],
        compiler_params=pltpu.CompilerParams(
            collective_id=0, has_side_effects=True, vmem_limit_bytes=60 * 1024 * 1024
        ),
    )(
        image,
        inverse_var,
        patch_of.reshape(1, wide),
        row_of.reshape(1, wide),
        valid.reshape(1, wide),
        coef_index.reshape(1, count),
        coef_table.T,
        basis_across,
        basis_down,
    )


def solution(mesh):
    placed = (
        P(("skyx", "skyy"), None, None),
        P(("skyx", "skyy"), None, None),
        P(),
        P(),
        P(),
        P(),
        P(),
        P(),
        P(),
    )
    return jax.shard_map(
        body,
        mesh=mesh,
        in_specs=placed,
        out_specs=(P("skyy", "skyx"), P("skyy", "skyx")),
        check_vma=False,
    )
```

time: 44.4 us -> 34.1 us (0.77)
  local copies, waits for them, and re-layouts: 6.98 us -> 2.26 us
  Pallas kernels: 35.1 us -> 30.6 us
  other arithmetic: 1 us -> 0 us
    pallas_call x1, Pallas kernels: 35.1 us -> 30.6 us  [body(): pl.pallas_call(functools.partial(kernel, nx, ny, taps), out_shape=(jax.Sh...]
    unnamed x22 -> x4, local copies, waits for them, and re-layouts: 6.5 us -> 2.26 us
    unnamed x1 -> x0, other arithmetic: 0.68 us -> none
where the time goes in v2:
time: 34.1 us; the launch traced here: 33.5 us
  Pallas kernels  30.6 us (90%)
  local copies, waits for them, and re-layouts  2.26 us (7%)
  between operations  0.65 us (2%)
    pallas_call x1, Pallas kernels, body(): pl.pallas_call(functools.partial(kernel, nx, ny, taps), out_shape=(jax.Sh...  30.6 us
    unnamed x4, local copies, waits for them, and re-layouts  2.26 us

profile of v2, /device:TPU:0, one launch (start us, length us, event | category | flops | bytes accessed | tf_op | source)
XLA Modules:
  0.0 33.5 jit_solution(3455106623831566804)
XLA Ops:
  0.6 30.6 %shard_map.104 = (f32[64,512]{1,0:T(8,128)}, f32[64,512]{1,0:T(8,128)}) custom-call(bf16[16,16,512]{2,1,0:T(8,128)(2,1)} %image_hbm.1, bf16[16,16,512]{2,1,0:T(8,128)(2,1)} %ivar_hbm.1, s32[1,512]{1,0:T(1,128)} %bitcast.6, s32[1,512]{1,0:T(1,128)} %bitcast.7, s32[1,512]{1,0:T(1,128)} %bitcast.8, s32[1,32]{1,0:T(1,128)} %bitcast.9, f32[20,64]{1,0:T(8,128)} %bitcast.5, ...), custom_call_target="tpu_custom_call" | custom-call | tf_op jit(solution)/shard_map/pallas_call | solution.py:450
  31.2 0.0 copy-start
  31.3 1.6 %copy.13 = f32[64,512]{1,0:T(8,128)} copy(f32[64,512]{1,0:T(8,128)} %get-tuple-element.4) | data formatting | bytes 262144
  32.9 0.0 copy-done
  32.9 0.7 %copy.14 = f32[64,512]{1,0:T(8,128)} copy(f32[64,512]{1,0:T(8,128)S(1)} %copy-done) | data formatting | bytes 262144
Async XLA Ops:
  31.2 1.6 %copy-start = (f32[64,512]{1,0:T(8,128)S(1)}, f32[64,512]{1,0:T(8,128)}, u32[]{:S(2)}) copy-start(f32[64,512]{1,0:T(8,128)} %get-tuple-element.5) | copy-start | bytes 393220

commit v3 on v2

--- a/solution.py
+++ b/solution.py
@@ -51,6 +51,7 @@
     coef_rows,
     chosen,
     bands,
+    shifts,
     mixer,
     mixed_tiles,
     ext,
@@ -130,7 +131,6 @@
         product = weight.astype(jnp.float32) * image_ref[block].astype(jnp.float32)
         send[patch] = product.astype(jnp.bfloat16)
         keep_send[tx * INNER + tlo, thi] = weight
-        return patch
 
     def block_copy(target, source, device):
         return pltpu.make_async_remote_copy(
@@ -162,16 +162,20 @@
             device_id_type=MESH,
         )
 
+    def prepare(step, carry):
+        stage(*partner(step))
+        return carry
+
+    lax.fori_loop(0, count, prepare, 0)
     pl.semaphore_wait(barrier, count - 1)
 
     def start(step, carry):
         tx, thi, tlo = partner(step)
-        patch = stage(tx, thi, tlo)
-        block_copy(patch, me, (tx, thi * INNER + tlo)).start()
+        ty = thi * INNER + tlo
+        block_copy(tx * ny + ty, me, (tx, ty)).start()
         return carry
 
     lax.fori_loop(0, count - 1, start, 0)
-    stage(mx, hi, lo)
     recv[me] = send[me]
 
     def member_of(step):
@@ -189,17 +193,17 @@
     for load in loads[3:]:
         load.wait()
 
-    across_pad[...] = jnp.zeros_like(across_pad)
-    across_pad[:, :taps] = across_ref[...]
-    down_pad[...] = jnp.zeros_like(down_pad)
-    down_pad[:, :taps] = down_ref[...]
-    down_pad[...] = pltpu.roll(down_pad[...], LEAD, 1)
-
     def same(condition):
         return condition.astype(jnp.float32).astype(jnp.bfloat16)
 
     def iota(shape, dim):
         return lax.broadcasted_iota(jnp.int32, shape, dim)
+
+    def over(value, by):
+        return value >> (by.bit_length() - 1) if by & (by - 1) == 0 else value // by
+
+    def within(value, by):
+        return value & (by - 1) if by & (by - 1) == 0 else lax.rem(value, by)
 
     def spread(slots, groups):
         lanes = slots.shape[1]
@@ -207,7 +211,7 @@
             [jnp.broadcast_to(slots[s : s + 1], (rows, lanes)) for s in range(groups * RS)], axis=0
         )
         shape = tall_flags.shape
-        keep = lax.rem(iota(shape, 0), rows) == lax.rem(iota(shape, 1), rows)
+        keep = within(iota(shape, 0), rows) == within(iota(shape, 1), rows)
         return jnp.where(keep, tall_flags, 0.0).astype(jnp.bfloat16)
 
     spot = jnp.where(valid_lanes[...] > 0, patch_lanes[...] * RS + row_lanes[...], -1)
@@ -216,7 +220,7 @@
     own_slots = jnp.where(iota((8, wide), 0) < RS, own_slots, jnp.bfloat16(0))
     chunk = LANES // rows
     repeat = same(
-        iota((chunk * blocks, LANES), 0) // blocks == iota((chunk * blocks, LANES), 1) // rows
+        over(iota((chunk * blocks, LANES), 0), blocks) == over(iota((chunk * blocks, LANES), 1), rows)
     )
     own_flags = jnp.concatenate(
         [
@@ -243,43 +247,72 @@
     deep = count * rows
     coef_rows[...] = jnp.dot(
         coeffs,
-        (iota((count, deep), 0) == iota((count, deep), 1) // rows).astype(jnp.float32),
+        (iota((count, deep), 0) == over(iota((count, deep), 1), rows)).astype(jnp.float32),
         precision=lax.Precision.HIGHEST,
         preferred_element_type=jnp.float32,
     )
 
     shape = (planes * RS, wide)
-    wanted = (mx * ny + (iota(shape, 0) // RS) * INNER + lo) * RS + lax.rem(iota(shape, 0), RS)
+    wanted = (mx * ny + over(iota(shape, 0), RS) * INNER + lo) * RS + within(iota(shape, 0), RS)
     shape = (wide, members * rows)
-    member = iota(shape, 1) // rows
-    exposure = (member // INNER) * ny + hi * INNER + lax.rem(member, INNER)
+    member = over(iota(shape, 1), rows)
+    exposure = over(member, INNER) * ny + hi * INNER + within(member, INNER)
     plane_flags = jnp.dot(
         same(wanted == spot),
-        same(iota(shape, 0) // blocks == exposure),
+        same(over(iota(shape, 0), blocks) == exposure),
         preferred_element_type=jnp.float32,
     )
     plane_rows = spread(plane_flags, planes)
 
-    def build(channel, carry):
-        row = jnp.broadcast_to(across_pad[pl.ds(channel, 1), :], (LANES, 2 * LANES))
+    tap = iota((taps, LANES), 0)
+    lane = iota((taps, LANES), 1)
+
+    def laid(filters, where_to):
+        return jnp.dot(
+            filters,
+            (lane == where_to).astype(jnp.float32),
+            precision=lax.Precision.HIGHEST,
+            preferred_element_type=jnp.float32,
+        )
+
+    across_pad[...] = laid(across_ref[...], tap)
+    down_pad[...] = laid(down_ref[...], LANES - LEAD - tap)
+    forward = iota((LANES, LANES), 1) >= iota((LANES, LANES), 0)
+    first_half = iota((tall, LANES), 1) < patch_rows
+
+    def build_bands(channel, carry):
+        row = jnp.broadcast_to(across_pad[pl.ds(channel, 1), :], (LANES, LANES))
         band = pltpu.roll(row, 0, 1, stride=1, stride_axis=0)
-        bands[pl.ds(pl.multiple_of(channel * LANES, LANES), LANES), :] = band.astype(jnp.bfloat16)
-        row = jnp.broadcast_to(down_pad[pl.ds(channel, 1), :], (patch_rows, LANES))
+        start_row = pl.multiple_of(channel * LANES, LANES)
+        bands[pl.ds(start_row, LANES), :LANES] = jnp.where(forward, band, 0.0).astype(jnp.bfloat16)
+        bands[pl.ds(start_row, LANES), LANES:] = jnp.where(forward, 0.0, band).astype(jnp.bfloat16)
+        row = jnp.broadcast_to(down_pad[pl.ds(channel, 1), :], (tall, LANES))
         shifted = pltpu.roll(row, 0, 1, stride=1, stride_axis=0)
-        high = shifted.astype(jnp.bfloat16)
-        low = (shifted - high.astype(jnp.float32)).astype(jnp.bfloat16)
-        picked = lax.dot_general(
-            jnp.concatenate([high, low], axis=0),
+        high = shifted.astype(jnp.bfloat16).astype(jnp.float32)
+        low = pltpu.roll(shifted - high, patch_rows, 1)
+        start_row = pl.multiple_of(channel * tall, 16)
+        shifts[pl.ds(start_row, tall), :] = jnp.where(first_half, high, low).astype(jnp.bfloat16)
+        return carry
+
+    lax.fori_loop(0, channels, build_bands, 0, unroll=4)
+
+    def build_mixer(turn, carry):
+        start_row = pl.multiple_of(turn * GROUP * tall, 16)
+        picked = jnp.dot(
+            shifts[pl.ds(start_row, GROUP * tall), :],
             chosen[...],
-            (((0,), (0,)), ((), ())),
             preferred_element_type=jnp.float32,
         )
-        mixed = picked[:tall] * coef_rows[pl.ds(channel, 1), :]
-        start_row = pl.multiple_of(channel * tall, 16)
-        mixer[pl.ds(start_row, tall), :] = mixed.astype(jnp.bfloat16)
-        return carry
-
-    lax.fori_loop(0, channels, build, 0)
+        for member in range(GROUP):
+            mixed = picked[member * tall : (member + 1) * tall] * coef_rows[
+                pl.ds(turn * GROUP + member, 1), :
+            ]
+            mixer[pl.ds(pl.multiple_of(start_row + member * tall, 16), tall), :] = mixed.astype(
+                jnp.bfloat16
+            )
+        return carry
+
+    lax.fori_loop(0, channels // GROUP, build_mixer, 0)
 
     def wait_keep(step, carry):
         tx, tlo = member_of(step)
@@ -445,7 +478,18 @@
     wide = count * blocks
 
     vmem = pl.BlockSpec(memory_space=pltpu.VMEM)
-    anywhere = pl.BlockSpec(memory_space=pl.ANY)
+    operands = [
+        image,
+        inverse_var,
+        patch_of.reshape(1, wide),
+        row_of.reshape(1, wide),
+        valid.reshape(1, wide),
+        coef_index.reshape(1, count),
+        coef_table.T,
+        basis_across,
+        basis_down,
+    ]
+    in_hbm = pl.BlockSpec(memory_space=pltpu.HBM)
     dma = pltpu.SemaphoreType.DMA
     return pl.pallas_call(
         functools.partial(kernel, nx, ny, taps),
@@ -453,7 +497,7 @@
             jax.ShapeDtypeStruct((patch_rows, width), jnp.float32),
             jax.ShapeDtypeStruct((patch_rows, width), jnp.float32),
         ),
-        in_specs=[anywhere] * 9,
+        in_specs=[in_hbm] * len(operands),
         out_specs=(vmem, vmem),
         scratch_shapes=[
             pltpu.VMEM((blocks, rows, width), jnp.bfloat16),
@@ -472,11 +516,12 @@
             pltpu.VMEM((members, planes, rows, width), jnp.bfloat16),
             pltpu.VMEM((planes, patch_rows, width), jnp.bfloat16),
             pltpu.VMEM((planes, patch_rows, width), jnp.bfloat16),
-            pltpu.VMEM((channels, 2 * LANES), jnp.float32),
+            pltpu.VMEM((channels, LANES), jnp.float32),
             pltpu.VMEM((channels, LANES), jnp.float32),
             pltpu.VMEM((channels, deep), jnp.float32),
             pltpu.VMEM((2 * patch_rows, deep), jnp.bfloat16),
             pltpu.VMEM((channels * LANES, 2 * LANES), jnp.bfloat16),
+            pltpu.VMEM((channels * tall, LANES), jnp.bfloat16),
             pltpu.VMEM((channels * tall, deep), jnp.bfloat16),
             pltpu.VMEM((tiles * tall, channels * LANES), jnp.bfloat16),
             pltpu.VMEM((tall, width + LANES), jnp.float32),
@@ -494,19 +539,9 @@
             dma((8,)),
         ],
         compiler_params=pltpu.CompilerParams(
-            collective_id=0, has_side_effects=True, vmem_limit_bytes=60 * 1024 * 1024
+            collective_id=0, has_side_effects=True, vmem_limit_bytes=(16 * 1024 + 256 * count) * 1024
         ),
-    )(
-        image,
-        inverse_var,
-        patch_of.reshape(1, wide),
-        row_of.reshape(1, wide),
-        valid.reshape(1, wide),
-        coef_index.reshape(1, count),
-        coef_table.T,
-        basis_across,
-        basis_down,
-    )
+    )(*[pltpu.with_memory_space_constraint(operand, pltpu.HBM) for operand in operands])
 
 
 def solution(mesh):

time: 34.1 us -> 32 us (0.938)
  Pallas kernels: 30.6 us -> 29.5 us
  local copies, waits for them, and re-layouts: 2.26 us -> 1.31 us
    pallas_call x1, Pallas kernels: 30.6 us -> 29.5 us  [body(): pl.pallas_call(functools.partial(kernel, nx, ny, taps), out_shape=(jax.Sh...]
    unnamed x4 -> x2, local copies, waits for them, and re-layouts: 2.26 us -> 1.31 us
where the time goes in v3:
time: 32 us; the launch traced here: 31.5 us
  Pallas kernels  29.5 us (92%)
  local copies, waits for them, and re-layouts  1.31 us (4%)
  between operations  0.64 us (2%)
    pallas_call x1, Pallas kernels, body(): pl.pallas_call(functools.partial(kernel, nx, ny, taps), out_shape=(jax.Sh...  29.5 us
    unnamed x2, local copies, waits for them, and re-layouts  1.31 us

profile of v3, /device:TPU:0, one launch (start us, length us, event | category | flops | bytes accessed | tf_op | source)
XLA Modules:
  0.0 31.5 jit_solution(18135042168774730074)
XLA Ops:
  0.6 29.5 %shard_map.104 = (f32[64,512]{1,0:T(8,128)S(1)}, f32[64,512]{1,0:T(8,128)S(1)}) custom-call(bf16[16,16,512]{2,1,0:T(8,128)(2,1)} %image_hbm.1, bf16[16,16,512]{2,1,0:T(8,128)(2,1)} %ivar_hbm.1, s32[1,512]{1,0:T(1,128)} %bitcast.6, s32[1,512]{1,0:T(1,128)} %bitcast.7, s32[1,512]{1,0:T(1,128)} %bitcast.8, s32[1,32]{1,0:T(1,128)} %bitcast.9, f32[20,64]{1,0:T(8,128)} %bitcast.5, ...), custom_call_target="tpu_custom_call" | custom-call | tf_op jit(solution)/shard_map/pallas_call | solution.py:494
  30.2 0.7 %copy.13 = f32[64,512]{1,0:T(8,128)} copy(f32[64,512]{1,0:T(8,128)S(1)} %get-tuple-element.4) | data formatting | bytes 262144
  30.8 0.7 %copy.14 = f32[64,512]{1,0:T(8,128)} copy(f32[64,512]{1,0:T(8,128)S(1)} %get-tuple-element.5) | data formatting | bytes 262144

commit v4 on v3

--- a/solution.py
+++ b/solution.py
@@ -45,6 +45,8 @@
     keep_send,
     keep_recv,
     part_send,
+    pair_recv,
+    merged,
     part_recv,
     across_pad,
     down_pad,
@@ -63,6 +65,7 @@
     recv_sem,
     keep_send_sem,
     keep_recv_sem,
+    pair_sem,
     part_send_sem,
     part_recv_sem,
     edge_send_sem,
@@ -152,9 +155,22 @@
             device_id_type=MESH,
         )
 
+    half = planes // 2
+    parity, rank = lax.rem(hi, 2), hi // 2
+
+    def pair_copy():
+        return pltpu.make_async_remote_copy(
+            src_ref=part_send.at[1 - parity],
+            dst_ref=pair_recv,
+            send_sem=pair_sem.at[0],
+            recv_sem=pair_sem.at[1],
+            device_id=(mx, (hi + 1 - 2 * parity) * INNER + lo),
+            device_id_type=MESH,
+        )
+
     def part_copy(target, source, device):
         return pltpu.make_async_remote_copy(
-            src_ref=part_send.at[target],
+            src_ref=merged.at[target],
             dst_ref=part_recv.at[source],
             send_sem=part_send_sem.at[target],
             recv_sem=part_recv_sem.at[source],
@@ -175,8 +191,7 @@
         block_copy(tx * ny + ty, me, (tx, ty)).start()
         return carry
 
-    lax.fori_loop(0, count - 1, start, 0)
-    recv[me] = send[me]
+    lax.fori_loop(0, count - members, start, 0)
 
     def member_of(step):
         return lax.rem(mx + step // INNER, nx), lax.rem(lo + lax.rem(step, INNER), INNER)
@@ -189,6 +204,8 @@
         return carry
 
     lax.fori_loop(1, members, start_keep, 0)
+    lax.fori_loop(count - members, count - 1, start, 0)
+    recv[me] = send[me]
     keep_recv[own_member] = keep_send[own_member]
     for load in loads[3:]:
         load.wait()
@@ -321,12 +338,12 @@
 
     lax.fori_loop(1, members, wait_keep, 0)
     for plane in range(planes):
-        part_send[plane] = jnp.dot(
+        part_send[plane % 2, plane // 2] = jnp.dot(
             plane_rows[plane * patch_rows : (plane + 1) * patch_rows],
             keep_recv[:, plane].reshape(members * rows, width),
             preferred_element_type=jnp.float32,
         ).astype(jnp.bfloat16)
-    part_recv[hi] = part_send[hi]
+    pair_copy().start()
 
     def wait_block(step, carry):
         tx, thi, tlo = partner(step)
@@ -336,15 +353,25 @@
 
     lax.fori_loop(0, count - 1, wait_block, 0)
 
-    def plane_at(step):
-        return lax.rem(hi + step, planes)
+    pair_copy().wait_recv()
+    for place in range(half):
+        merged[place] = (
+            part_send[parity, place].astype(jnp.float32) + pair_recv[place].astype(jnp.float32)
+        ).astype(jnp.bfloat16)
+    part_recv[rank] = merged[rank]
+
+    def rank_at(step):
+        return lax.rem(rank + step, half)
+
+    def device_at(place):
+        return (mx, (place * 2 + parity) * INNER + lo)
 
     def start_part(step, carry):
-        thi = plane_at(step)
-        part_copy(thi, hi, (mx, thi * INNER + lo)).start()
-        return carry
-
-    lax.fori_loop(1, planes, start_part, 0)
+        place = rank_at(step)
+        part_copy(place, rank, device_at(place)).start()
+        return carry
+
+    lax.fori_loop(1, half, start_part, 0)
     arrived = recv[...].reshape(deep, width)
     for turn in range(channels // GROUP):
         mixed = jnp.dot(
@@ -400,15 +427,35 @@
 
     coadd_ref[...] = ext[middle, body_cols]
 
+    def sent_block(step, carry):
+        tx, thi, tlo = partner(step)
+        ty = thi * INNER + tlo
+        block_copy(tx * ny + ty, me, (tx, ty)).wait_send()
+        return carry
+
+    def sent_keep(step, carry):
+        tx, tlo = member_of(step)
+        keep_copy(tx * INNER + tlo, own_member, (tx, hi * INNER + tlo)).wait_send()
+        return carry
+
+    def sent_part(step, carry):
+        place = rank_at(step)
+        part_copy(place, rank, device_at(place)).wait_send()
+        return carry
+
+    lax.fori_loop(0, count - 1, sent_block, 0)
+    lax.fori_loop(1, members, sent_keep, 0)
+    pair_copy().wait_send()
+    lax.fori_loop(1, half, sent_part, 0)
     def wait_part(step, carry):
-        thi = plane_at(step)
-        part_copy(hi, thi, (mx, thi * INNER + lo)).wait_recv()
-        return carry
-
-    lax.fori_loop(1, planes, wait_part, 0)
+        place = rank_at(step)
+        part_copy(rank, place, device_at(place)).wait_recv()
+        return carry
+
+    lax.fori_loop(1, half, wait_part, 0)
     weights = part_recv[0].astype(jnp.float32)
-    for plane in range(1, planes):
-        weights = weights + part_recv[plane].astype(jnp.float32)
+    for place in range(1, half):
+        weights = weights + part_recv[place].astype(jnp.float32)
     weight_ref[...] = weights
 
     lane = lax.broadcasted_iota(jnp.int32, (spill, LANES), 1)
@@ -435,25 +482,6 @@
                 here = (low_rows if dy > 0 else high_rows, left if dx > 0 else right)
                 coadd_ref[here] += from_side(landing[...], lane, -dx)
 
-    def sent_block(step, carry):
-        tx, thi, tlo = partner(step)
-        ty = thi * INNER + tlo
-        block_copy(tx * ny + ty, me, (tx, ty)).wait_send()
-        return carry
-
-    def sent_keep(step, carry):
-        tx, tlo = member_of(step)
-        keep_copy(tx * INNER + tlo, own_member, (tx, hi * INNER + tlo)).wait_send()
-        return carry
-
-    def sent_part(step, carry):
-        thi = plane_at(step)
-        part_copy(thi, hi, (mx, thi * INNER + lo)).wait_send()
-        return carry
-
-    lax.fori_loop(0, count - 1, sent_block, 0)
-    lax.fori_loop(1, members, sent_keep, 0)
-    lax.fori_loop(1, planes, sent_part, 0)
     for number, (dx, dy, _, _) in enumerate(plan):
 
         @pl.when(exists(dx, dy))
@@ -514,8 +542,10 @@
             pltpu.VMEM((count, rows, width), jnp.bfloat16),
             pltpu.VMEM((members, planes, rows, width), jnp.bfloat16),
             pltpu.VMEM((members, planes, rows, width), jnp.bfloat16),
-            pltpu.VMEM((planes, patch_rows, width), jnp.bfloat16),
-            pltpu.VMEM((planes, patch_rows, width), jnp.bfloat16),
+            pltpu.VMEM((2, planes // 2, patch_rows, width), jnp.bfloat16),
+            pltpu.VMEM((planes // 2, patch_rows, width), jnp.bfloat16),
+            pltpu.VMEM((planes // 2, patch_rows, width), jnp.bfloat16),
+            pltpu.VMEM((planes // 2, patch_rows, width), jnp.bfloat16),
             pltpu.VMEM((channels, LANES), jnp.float32),
             pltpu.VMEM((channels, LANES), jnp.float32),
             pltpu.VMEM((channels, deep), jnp.float32),
@@ -533,8 +563,9 @@
             dma((count,)),
             dma((members,)),
             dma((members,)),
-            dma((planes,)),
-            dma((planes,)),
+            dma((2,)),
+            dma((planes // 2,)),
+            dma((planes // 2,)),
             dma((8,)),
             dma((8,)),
         ],

time: 32 us -> 32.1 us (level); the launches traced: 31.5 us -> 32 us
  Pallas kernels: 29.5 us -> 30 us
    pallas_call x1, Pallas kernels: 29.5 us -> 30 us  [body(): pl.pallas_call(functools.partial(kernel, nx, ny, taps), out_shape=(jax.Sh...]
where the time goes in v4:
time: 32.1 us; the launch traced here: 32 us
  Pallas kernels  30 us (93%)
  local copies, waits for them, and re-layouts  1.31 us (4%)
  between operations  0.64 us (2%)
    pallas_call x1, Pallas kernels, body(): pl.pallas_call(functools.partial(kernel, nx, ny, taps), out_shape=(jax.Sh...  30 us
    unnamed x2, local copies, waits for them, and re-layouts  1.31 us

profile of v4, /device:TPU:0, one launch (start us, length us, event | category | flops | bytes accessed | tf_op | source)
XLA Modules:
  0.0 32.0 jit_solution(490022407914483274)
XLA Ops:
  0.6 30.0 %shard_map.104 = (f32[64,512]{1,0:T(8,128)S(1)}, f32[64,512]{1,0:T(8,128)S(1)}) custom-call(bf16[16,16,512]{2,1,0:T(8,128)(2,1)} %image_hbm.1, bf16[16,16,512]{2,1,0:T(8,128)(2,1)} %ivar_hbm.1, s32[1,512]{1,0:T(1,128)} %bitcast.6, s32[1,512]{1,0:T(1,128)} %bitcast.7, s32[1,512]{1,0:T(1,128)} %bitcast.8, s32[1,32]{1,0:T(1,128)} %bitcast.9, f32[20,64]{1,0:T(8,128)} %bitcast.5, ...), custom_call_target="tpu_custom_call" | custom-call | tf_op jit(solution)/shard_map/pallas_call | solution.py:522
  30.7 0.7 %copy.13 = f32[64,512]{1,0:T(8,128)} copy(f32[64,512]{1,0:T(8,128)S(1)} %get-tuple-element.4) | data formatting | bytes 262144
  31.3 0.7 %copy.14 = f32[64,512]{1,0:T(8,128)} copy(f32[64,512]{1,0:T(8,128)S(1)} %get-tuple-element.5) | data formatting | bytes 262144

commit v5 on v4

--- a/solution.py
+++ b/solution.py
@@ -33,6 +33,7 @@
     image_ref,
     ivar_ref,
     patch_scalars,
+    picks,
     patch_lanes,
     row_lanes,
     valid_lanes,
@@ -121,15 +122,23 @@
         return carry
 
     lax.fori_loop(0, count - 1, greet, 0)
-    for load in loads[:3]:
-        load.wait()
+    loads[0].wait()
     targets = [patch_scalars[0, me * blocks + k] for k in range(blocks)]
 
-    def stage(tx, thi, tlo):
-        patch = tx * ny + thi * INNER + tlo
+    def find(patch, carry):
         block = 0
         for k in range(1, blocks):
             block = jnp.where(targets[k] == patch, k, block)
+        picks[patch] = block
+        return carry
+
+    lax.fori_loop(0, count, find, 0)
+    for load in loads[1:3]:
+        load.wait()
+
+    def stage(tx, thi, tlo):
+        patch = tx * ny + thi * INNER + tlo
+        block = picks[patch]
         weight = ivar_ref[block]
         product = weight.astype(jnp.float32) * image_ref[block].astype(jnp.float32)
         send[patch] = product.astype(jnp.bfloat16)
@@ -353,25 +362,6 @@
 
     lax.fori_loop(0, count - 1, wait_block, 0)
 
-    pair_copy().wait_recv()
-    for place in range(half):
-        merged[place] = (
-            part_send[parity, place].astype(jnp.float32) + pair_recv[place].astype(jnp.float32)
-        ).astype(jnp.bfloat16)
-    part_recv[rank] = merged[rank]
-
-    def rank_at(step):
-        return lax.rem(rank + step, half)
-
-    def device_at(place):
-        return (mx, (place * 2 + parity) * INNER + lo)
-
-    def start_part(step, carry):
-        place = rank_at(step)
-        part_copy(place, rank, device_at(place)).start()
-        return carry
-
-    lax.fori_loop(1, half, start_part, 0)
     arrived = recv[...].reshape(deep, width)
     for turn in range(channels // GROUP):
         mixed = jnp.dot(
@@ -427,6 +417,25 @@
 
     coadd_ref[...] = ext[middle, body_cols]
 
+    pair_copy().wait_recv()
+    for place in range(half):
+        merged[place] = (
+            part_send[parity, place].astype(jnp.float32) + pair_recv[place].astype(jnp.float32)
+        ).astype(jnp.bfloat16)
+    part_recv[rank] = merged[rank]
+
+    def rank_at(step):
+        return lax.rem(rank + step, half)
+
+    def device_at(place):
+        return (mx, (place * 2 + parity) * INNER + lo)
+
+    def start_part(step, carry):
+        place = rank_at(step)
+        part_copy(place, rank, device_at(place)).start()
+        return carry
+
+    lax.fori_loop(1, half, start_part, 0)
     def sent_block(step, carry):
         tx, thi, tlo = partner(step)
         ty = thi * INNER + tlo
@@ -438,26 +447,9 @@
         keep_copy(tx * INNER + tlo, own_member, (tx, hi * INNER + tlo)).wait_send()
         return carry
 
-    def sent_part(step, carry):
-        place = rank_at(step)
-        part_copy(place, rank, device_at(place)).wait_send()
-        return carry
-
     lax.fori_loop(0, count - 1, sent_block, 0)
     lax.fori_loop(1, members, sent_keep, 0)
     pair_copy().wait_send()
-    lax.fori_loop(1, half, sent_part, 0)
-    def wait_part(step, carry):
-        place = rank_at(step)
-        part_copy(rank, place, device_at(place)).wait_recv()
-        return carry
-
-    lax.fori_loop(1, half, wait_part, 0)
-    weights = part_recv[0].astype(jnp.float32)
-    for place in range(1, half):
-        weights = weights + part_recv[place].astype(jnp.float32)
-    weight_ref[...] = weights
-
     lane = lax.broadcasted_iota(jnp.int32, (spill, LANES), 1)
     lane_tall = lax.broadcasted_iota(jnp.int32, (patch_rows, LANES), 1)
     low_rows, high_rows = pl.ds(0, spill), pl.ds(patch_rows - spill, spill)
@@ -482,6 +474,23 @@
                 here = (low_rows if dy > 0 else high_rows, left if dx > 0 else right)
                 coadd_ref[here] += from_side(landing[...], lane, -dx)
 
+    def sent_part(step, carry):
+        place = rank_at(step)
+        part_copy(place, rank, device_at(place)).wait_send()
+        return carry
+
+    def wait_part(step, carry):
+        place = rank_at(step)
+        part_copy(rank, place, device_at(place)).wait_recv()
+        return carry
+
+    lax.fori_loop(1, half, wait_part, 0)
+    weights = part_recv[0].astype(jnp.float32)
+    for place in range(1, half):
+        weights = weights + part_recv[place].astype(jnp.float32)
+    weight_ref[...] = weights
+
+    lax.fori_loop(1, half, sent_part, 0)
     for number, (dx, dy, _, _) in enumerate(plan):
 
         @pl.when(exists(dx, dy))
@@ -531,6 +540,7 @@
             pltpu.VMEM((blocks, rows, width), jnp.bfloat16),
             pltpu.VMEM((blocks, rows, width), jnp.bfloat16),
             pltpu.SMEM((1, wide), jnp.int32),
+            pltpu.SMEM((count,), jnp.int32),
             pltpu.VMEM((1, wide), jnp.int32),
             pltpu.VMEM((1, wide), jnp.int32),
             pltpu.VMEM((1, wide), jnp.int32),

time: 32.1 us -> 32.2 us (level)
  no operation moved by 1% of the time
where the time goes in v5:
time: 32.2 us; the launch traced here: 32.1 us
  Pallas kernels  30.1 us (93%)
  local copies, waits for them, and re-layouts  1.31 us (4%)
  between operations  0.64 us (2%)
    pallas_call x1, Pallas kernels, body(): pl.pallas_call(functools.partial(kernel, nx, ny, taps), out_shape=(jax.Sh...  30.1 us
    unnamed x2, local copies, waits for them, and re-layouts  1.31 us

profile of v5, /device:TPU:0, one launch (start us, length us, event | category | flops | bytes accessed | tf_op | source)
XLA Modules:
  0.0 32.1 jit_solution(16197901999512243076)
XLA Ops:
  0.6 30.1 %shard_map.104 = (f32[64,512]{1,0:T(8,128)S(1)}, f32[64,512]{1,0:T(8,128)S(1)}) custom-call(bf16[16,16,512]{2,1,0:T(8,128)(2,1)} %image_hbm.1, bf16[16,16,512]{2,1,0:T(8,128)(2,1)} %ivar_hbm.1, s32[1,512]{1,0:T(1,128)} %bitcast.6, s32[1,512]{1,0:T(1,128)} %bitcast.7, s32[1,512]{1,0:T(1,128)} %bitcast.8, s32[1,32]{1,0:T(1,128)} %bitcast.9, f32[20,64]{1,0:T(8,128)} %bitcast.5, ...), custom_call_target="tpu_custom_call" | custom-call | tf_op jit(solution)/shard_map/pallas_call | solution.py:531
  30.8 0.7 %copy.13 = f32[64,512]{1,0:T(8,128)} copy(f32[64,512]{1,0:T(8,128)S(1)} %get-tuple-element.4) | data formatting | bytes 262144
  31.4 0.7 %copy.14 = f32[64,512]{1,0:T(8,128)} copy(f32[64,512]{1,0:T(8,128)S(1)} %get-tuple-element.5) | data formatting | bytes 262144

commit v6 on v5

--- a/solution.py
+++ b/solution.py
@@ -87,10 +87,19 @@
     me = mx * ny + my
     hi, lo = my // INNER, lax.rem(my, INNER)
 
+    def plane_across(distance):
+        if planes & (planes - 1):
+            return lax.rem(hi + distance, planes)
+        plane = 0
+        for bit in range(planes.bit_length() - 1):
+            power = 1 << bit
+            plane = plane + lax.rem(hi // power + distance // power, 2) * power
+        return plane
+
     def partner(step):
         back = count - 1 - step
         tx = lax.rem(mx + lax.rem(back // INNER, nx), nx)
-        thi = lax.rem(hi + back // members, planes)
+        thi = plane_across(back // members)
         tlo = lax.rem(lo + lax.rem(back, INNER), INNER)
         return tx, thi, tlo
 
@@ -200,7 +209,7 @@
         block_copy(tx * ny + ty, me, (tx, ty)).start()
         return carry
 
-    lax.fori_loop(0, count - members, start, 0)
+    lax.fori_loop(0, count // 2, start, 0)
 
     def member_of(step):
         return lax.rem(mx + step // INNER, nx), lax.rem(lo + lax.rem(step, INNER), INNER)
@@ -213,7 +222,7 @@
         return carry
 
     lax.fori_loop(1, members, start_keep, 0)
-    lax.fori_loop(count - members, count - 1, start, 0)
+    lax.fori_loop(count // 2, count - 1, start, 0)
     recv[me] = send[me]
     keep_recv[own_member] = keep_send[own_member]
     for load in loads[3:]:
@@ -375,6 +384,25 @@
                 mixed_tiles[
                     t * tall : (t + 1) * tall, channel * LANES : (channel + 1) * LANES
                 ] = mixed[member * tall : (member + 1) * tall, t * LANES : (t + 1) * LANES]
+    pair_copy().wait_recv()
+    for place in range(half):
+        merged[place] = (
+            part_send[parity, place].astype(jnp.float32) + pair_recv[place].astype(jnp.float32)
+        ).astype(jnp.bfloat16)
+    part_recv[rank] = merged[rank]
+
+    def rank_at(step):
+        return lax.rem(rank + step, half)
+
+    def device_at(place):
+        return (mx, (place * 2 + parity) * INNER + lo)
+
+    def start_part(step, carry):
+        place = rank_at(step)
+        part_copy(place, rank, device_at(place)).start()
+        return carry
+
+    lax.fori_loop(1, half, start_part, 0)
     summed = jnp.dot(mixed_tiles[...], bands[...], preferred_element_type=jnp.float32)
     zeros = jnp.zeros((tall, LANES), jnp.float32)
     now = [summed[t * tall : (t + 1) * tall, :LANES] for t in range(tiles)] + [zeros]
@@ -417,25 +445,6 @@
 
     coadd_ref[...] = ext[middle, body_cols]
 
-    pair_copy().wait_recv()
-    for place in range(half):
-        merged[place] = (
-            part_send[parity, place].astype(jnp.float32) + pair_recv[place].astype(jnp.float32)
-        ).astype(jnp.bfloat16)
-    part_recv[rank] = merged[rank]
-
-    def rank_at(step):
-        return lax.rem(rank + step, half)
-
-    def device_at(place):
-        return (mx, (place * 2 + parity) * INNER + lo)
-
-    def start_part(step, carry):
-        place = rank_at(step)
-        part_copy(place, rank, device_at(place)).start()
-        return carry
-
-    lax.fori_loop(1, half, start_part, 0)
     def sent_block(step, carry):
         tx, thi, tlo = partner(step)
         ty = thi * INNER + tlo
@@ -496,6 +505,15 @@
         @pl.when(exists(dx, dy))
         def _():
             edge_copy(number).wait_send()
+
+
+def hand_out(coadd_ref, weight_ref, coadd_out, weight_out, sem):
+    first = pltpu.make_async_copy(coadd_ref, coadd_out, sem.at[0])
+    second = pltpu.make_async_copy(weight_ref, weight_out, sem.at[1])
+    first.start()
+    second.start()
+    first.wait()
+    second.wait()
 
 
 def body(
@@ -528,7 +546,7 @@
     ]
     in_hbm = pl.BlockSpec(memory_space=pltpu.HBM)
     dma = pltpu.SemaphoreType.DMA
-    return pl.pallas_call(
+    outputs = pl.pallas_call(
         functools.partial(kernel, nx, ny, taps),
         out_shape=(
             jax.ShapeDtypeStruct((patch_rows, width), jnp.float32),
@@ -583,6 +601,13 @@
             collective_id=0, has_side_effects=True, vmem_limit_bytes=(16 * 1024 + 256 * count) * 1024
         ),
     )(*[pltpu.with_memory_space_constraint(operand, pltpu.HBM) for operand in operands])
+    return pl.pallas_call(
+        hand_out,
+        out_shape=tuple(jax.ShapeDtypeStruct(value.shape, value.dtype) for value in outputs),
+        in_specs=[vmem, vmem],
+        out_specs=(in_hbm, in_hbm),
+        scratch_shapes=[dma((2,))],
+    )(*outputs)
 
 
 def solution(mesh):

time: 32.2 us -> 33.2 us (1.031)
  Pallas kernels: 30.1 us -> 31.2 us
    pallas_call x0 -> x1, Pallas kernels: none -> 1.68 us  [body(): pl.pallas_call(hand_out, out_shape=tuple((jax.ShapeDtypeStruct(value.shap...]
    pallas_call x1, Pallas kernels: 30.1 us -> 29.5 us  [body(): pl.pallas_call(functools.partial(kernel, nx, ny, taps), out_shape=(jax.Sh...]
    unnamed x2 -> x4, local copies, waits for them, and re-layouts: 1.31 us -> 1.28 us
where the time goes in v6:
time: 33.2 us; the launch traced here: 33.1 us
  Pallas kernels  31.2 us (94%)
  local copies, waits for them, and re-layouts  1.28 us (4%)
  between operations  0.65 us (2%)
    pallas_call x1, Pallas kernels, body(): pl.pallas_call(functools.partial(kernel, nx, ny, taps), out_shape=(jax.Sh...  29.5 us
    pallas_call x1, Pallas kernels, body(): pl.pallas_call(hand_out, out_shape=tuple((jax.ShapeDtypeStruct(value.shap...  1.68 us
    unnamed x4, local copies, waits for them, and re-layouts  1.28 us

profile of v6, /device:TPU:0, one launch (start us, length us, event | category | flops | bytes accessed | tf_op | source)
XLA Modules:
  0.0 33.1 jit_solution(4531554437851869577)
XLA Ops:
  0.6 29.5 %shard_map.104 = (f32[64,512]{1,0:T(8,128)S(1)}, f32[64,512]{1,0:T(8,128)S(1)}) custom-call(bf16[16,16,512]{2,1,0:T(8,128)(2,1)} %image_hbm.1, bf16[16,16,512]{2,1,0:T(8,128)(2,1)} %ivar_hbm.1, s32[1,512]{1,0:T(1,128)} %bitcast.6, s32[1,512]{1,0:T(1,128)} %bitcast.7, s32[1,512]{1,0:T(1,128)} %bitcast.8, s32[1,32]{1,0:T(1,128)} %bitcast.9, f32[20,64]{1,0:T(8,128)} %bitcast.5, ...), custom_call_target="tpu_custom_call" | custom-call | tf_op jit(solution)/shard_map/pallas_call | solution.py:549
  30.1 0.0 copy-start
  30.1 0.6 %copy-done = f32[64,512]{1,0:T(8,128)} copy-done((f32[64,512]{1,0:T(8,128)}, f32[64,512]{1,0:T(8,128)S(1)}, u32[]{:S(2)}) %copy-start) | copy-done | bytes 131096
  30.8 0.0 copy-start.1
  30.8 0.6 %copy-done.1 = f32[64,512]{1,0:T(8,128)} copy-done((f32[64,512]{1,0:T(8,128)}, f32[64,512]{1,0:T(8,128)S(1)}, u32[]{:S(2)}) %copy-start.1) | copy-done | bytes 131096
  31.4 1.7 %shard_map.105 = (f32[64,512]{1,0:T(8,128)}, f32[64,512]{1,0:T(8,128)}) custom-call(f32[64,512]{1,0:T(8,128)} %copy-done, f32[64,512]{1,0:T(8,128)} %copy-done.1), custom_call_target="tpu_custom_call" | custom-call | tf_op jit(solution)/shard_map/pallas_call | solution.py:604
Async XLA Ops:
  30.1 0.6 %copy-start = (f32[64,512]{1,0:T(8,128)}, f32[64,512]{1,0:T(8,128)S(1)}, u32[]{:S(2)}) copy-start(f32[64,512]{1,0:T(8,128)S(1)} %get-tuple-element.4.coadd_ref) | copy-start | bytes 393220
  30.8 0.6 %copy-start.1 = (f32[64,512]{1,0:T(8,128)}, f32[64,512]{1,0:T(8,128)S(1)}, u32[]{:S(2)}) copy-start(f32[64,512]{1,0:T(8,128)S(1)} %get-tuple-element.5.weight_ref) | copy-start | bytes 393220

commit v7 on v5

--- a/solution.py
+++ b/solution.py
@@ -200,8 +200,6 @@
         block_copy(tx * ny + ty, me, (tx, ty)).start()
         return carry
 
-    lax.fori_loop(0, count - members, start, 0)
-
     def member_of(step):
         return lax.rem(mx + step // INNER, nx), lax.rem(lo + lax.rem(step, INNER), INNER)
 
@@ -213,7 +211,7 @@
         return carry
 
     lax.fori_loop(1, members, start_keep, 0)
-    lax.fori_loop(count - members, count - 1, start, 0)
+    lax.fori_loop(0, count - 1, start, 0)
     recv[me] = send[me]
     keep_recv[own_member] = keep_send[own_member]
     for load in loads[3:]:
@@ -242,6 +240,33 @@
 
     spot = jnp.where(valid_lanes[...] > 0, patch_lanes[...] * RS + row_lanes[...], -1)
     wide = count * blocks
+
+    shape = (planes * RS, wide)
+    wanted = (mx * ny + over(iota(shape, 0), RS) * INNER + lo) * RS + within(iota(shape, 0), RS)
+    shape = (wide, members * rows)
+    member = over(iota(shape, 1), rows)
+    exposure = over(member, INNER) * ny + hi * INNER + within(member, INNER)
+    plane_flags = jnp.dot(
+        same(wanted == spot),
+        same(over(iota(shape, 0), blocks) == exposure),
+        preferred_element_type=jnp.float32,
+    )
+    plane_rows = spread(plane_flags, planes)
+
+    def wait_keep(step, carry):
+        tx, tlo = member_of(step)
+        keep_copy(own_member, tx * INNER + tlo, (tx, hi * INNER + tlo)).wait_recv()
+        return carry
+
+    lax.fori_loop(1, members, wait_keep, 0)
+    for plane in range(planes):
+        part_send[plane % 2, plane // 2] = jnp.dot(
+            plane_rows[plane * patch_rows : (plane + 1) * patch_rows],
+            keep_recv[:, plane].reshape(members * rows, width),
+            preferred_element_type=jnp.float32,
+        ).astype(jnp.bfloat16)
+    pair_copy().start()
+
     own_slots = same(iota((8, wide), 0) + me * RS == spot)
     own_slots = jnp.where(iota((8, wide), 0) < RS, own_slots, jnp.bfloat16(0))
     chunk = LANES // rows
@@ -278,18 +303,6 @@
         preferred_element_type=jnp.float32,
     )
 
-    shape = (planes * RS, wide)
-    wanted = (mx * ny + over(iota(shape, 0), RS) * INNER + lo) * RS + within(iota(shape, 0), RS)
-    shape = (wide, members * rows)
-    member = over(iota(shape, 1), rows)
-    exposure = over(member, INNER) * ny + hi * INNER + within(member, INNER)
-    plane_flags = jnp.dot(
-        same(wanted == spot),
-        same(over(iota(shape, 0), blocks) == exposure),
-        preferred_element_type=jnp.float32,
-    )
-    plane_rows = spread(plane_flags, planes)
-
     tap = iota((taps, LANES), 0)
     lane = iota((taps, LANES), 1)
 
@@ -340,19 +353,25 @@
 
     lax.fori_loop(0, channels // GROUP, build_mixer, 0)
 
-    def wait_keep(step, carry):
-        tx, tlo = member_of(step)
-        keep_copy(own_member, tx * INNER + tlo, (tx, hi * INNER + tlo)).wait_recv()
-        return carry
-
-    lax.fori_loop(1, members, wait_keep, 0)
-    for plane in range(planes):
-        part_send[plane % 2, plane // 2] = jnp.dot(
-            plane_rows[plane * patch_rows : (plane + 1) * patch_rows],
-            keep_recv[:, plane].reshape(members * rows, width),
-            preferred_element_type=jnp.float32,
+    pair_copy().wait_recv()
+    for place in range(half):
+        merged[place] = (
+            part_send[parity, place].astype(jnp.float32) + pair_recv[place].astype(jnp.float32)
         ).astype(jnp.bfloat16)
-    pair_copy().start()
+    part_recv[rank] = merged[rank]
+
+    def rank_at(step):
+        return lax.rem(rank + step, half)
+
+    def device_at(place):
+        return (mx, (place * 2 + parity) * INNER + lo)
+
+    def start_part(step, carry):
+        place = rank_at(step)
+        part_copy(place, rank, device_at(place)).start()
+        return carry
+
+    lax.fori_loop(1, half, start_part, 0)
 
     def wait_block(step, carry):
         tx, thi, tlo = partner(step)
@@ -417,25 +436,6 @@
 
     coadd_ref[...] = ext[middle, body_cols]
 
-    pair_copy().wait_recv()
-    for place in range(half):
-        merged[place] = (
-            part_send[parity, place].astype(jnp.float32) + pair_recv[place].astype(jnp.float32)
-        ).astype(jnp.bfloat16)
-    part_recv[rank] = merged[rank]
-
-    def rank_at(step):
-        return lax.rem(rank + step, half)
-
-    def device_at(place):
-        return (mx, (place * 2 + parity) * INNER + lo)
-
-    def start_part(step, carry):
-        place = rank_at(step)
-        part_copy(place, rank, device_at(place)).start()
-        return carry
-
-    lax.fori_loop(1, half, start_part, 0)
     def sent_block(step, carry):
         tx, thi, tlo = partner(step)
         ty = thi * INNER + tlo

time: 32.2 us -> 33 us (1.025)
  Pallas kernels: 30.1 us -> 30.9 us
    pallas_call x1, Pallas kernels: 30.1 us -> 30.9 us  [body(): pl.pallas_call(functools.partial(kernel, nx, ny, taps), out_shape=(jax.Sh...]
where the time goes in v7:
time: 33 us; the launch traced here: 32.8 us
  Pallas kernels  30.9 us (94%)
  local copies, waits for them, and re-layouts  1.31 us (4%)
  between operations  0.64 us (2%)
    pallas_call x1, Pallas kernels, body(): pl.pallas_call(functools.partial(kernel, nx, ny, taps), out_shape=(jax.Sh...  30.9 us
    unnamed x2, local copies, waits for them, and re-layouts  1.31 us

profile of v7, /device:TPU:0, one launch (start us, length us, event | category | flops | bytes accessed | tf_op | source)
XLA Modules:
  0.0 32.8 jit_solution(9836690124888826024)
XLA Ops:
  0.6 30.9 %shard_map.104 = (f32[64,512]{1,0:T(8,128)S(1)}, f32[64,512]{1,0:T(8,128)S(1)}) custom-call(bf16[16,16,512]{2,1,0:T(8,128)(2,1)} %image_hbm.1, bf16[16,16,512]{2,1,0:T(8,128)(2,1)} %ivar_hbm.1, s32[1,512]{1,0:T(1,128)} %bitcast.6, s32[1,512]{1,0:T(1,128)} %bitcast.7, s32[1,512]{1,0:T(1,128)} %bitcast.8, s32[1,32]{1,0:T(1,128)} %bitcast.9, f32[20,64]{1,0:T(8,128)} %bitcast.5, ...), custom_call_target="tpu_custom_call" | custom-call | tf_op jit(solution)/shard_map/pallas_call | solution.py:531
  31.5 0.7 %copy.13 = f32[64,512]{1,0:T(8,128)} copy(f32[64,512]{1,0:T(8,128)S(1)} %get-tuple-element.4) | data formatting | bytes 262144
  32.2 0.7 %copy.14 = f32[64,512]{1,0:T(8,128)} copy(f32[64,512]{1,0:T(8,128)S(1)} %get-tuple-element.5) | data formatting | bytes 262144

commit v8 on v5

--- a/solution.py
+++ b/solution.py
@@ -87,10 +87,19 @@
     me = mx * ny + my
     hi, lo = my // INNER, lax.rem(my, INNER)
 
+    def plane_across(distance):
+        if planes & (planes - 1):
+            return lax.rem(hi + distance, planes)
+        plane = 0
+        for bit in range(planes.bit_length() - 1):
+            power = 1 << bit
+            plane = plane + lax.rem(hi // power + distance // power, 2) * power
+        return plane
+
     def partner(step):
         back = count - 1 - step
         tx = lax.rem(mx + lax.rem(back // INNER, nx), nx)
-        thi = lax.rem(hi + back // members, planes)
+        thi = plane_across(back // members)
         tlo = lax.rem(lo + lax.rem(back, INNER), INNER)
         return tx, thi, tlo
 

time: 32.2 us -> 32.7 us (1.016)
  Pallas kernels: 30.1 us -> 30.6 us
    pallas_call x1, Pallas kernels: 30.1 us -> 30.6 us  [body(): pl.pallas_call(functools.partial(kernel, nx, ny, taps), out_shape=(jax.Sh...]
where the time goes in v8:
time: 32.7 us; the launch traced here: 32.5 us
  Pallas kernels  30.6 us (94%)
  local copies, waits for them, and re-layouts  1.31 us (4%)
  between operations  0.64 us (2%)
    pallas_call x1, Pallas kernels, body(): pl.pallas_call(functools.partial(kernel, nx, ny, taps), out_shape=(jax.Sh...  30.6 us
    unnamed x2, local copies, waits for them, and re-layouts  1.31 us

profile of v8, /device:TPU:0, one launch (start us, length us, event | category | flops | bytes accessed | tf_op | source)
XLA Modules:
  0.0 32.5 jit_solution(5302621789880041431)
XLA Ops:
  0.6 30.6 %shard_map.104 = (f32[64,512]{1,0:T(8,128)S(1)}, f32[64,512]{1,0:T(8,128)S(1)}) custom-call(bf16[16,16,512]{2,1,0:T(8,128)(2,1)} %image_hbm.1, bf16[16,16,512]{2,1,0:T(8,128)(2,1)} %ivar_hbm.1, s32[1,512]{1,0:T(1,128)} %bitcast.6, s32[1,512]{1,0:T(1,128)} %bitcast.7, s32[1,512]{1,0:T(1,128)} %bitcast.8, s32[1,32]{1,0:T(1,128)} %bitcast.9, f32[20,64]{1,0:T(8,128)} %bitcast.5, ...), custom_call_target="tpu_custom_call" | custom-call | tf_op jit(solution)/shard_map/pallas_call | solution.py:540
  31.2 0.7 %copy.13 = f32[64,512]{1,0:T(8,128)} copy(f32[64,512]{1,0:T(8,128)S(1)} %get-tuple-element.4) | data formatting | bytes 262144
  31.9 0.7 %copy.14 = f32[64,512]{1,0:T(8,128)} copy(f32[64,512]{1,0:T(8,128)S(1)} %get-tuple-element.5) | data formatting | bytes 262144
